TPU v7x, 32 devices: a whole 2x2x4 slice. The times are simulated.
32 devices in a mesh: gx: 4 (over z), gy: 8 (over y, x, core).
Axes of the slice: x: 2, y: 2, z: 4, core: 2. Of those that a mesh axis runs over, the one named last changes fastest.
Arguments:
- rhs: float32 [4, 128, 256, 128], P(None, 'gx', 'gy'), may hold values from -4.5 to 4.5
- coefficient: float32 [4, 128, 256, 128], P(None, 'gx', 'gy'), may hold values from 0.01 to 0.3
Outputs:
- solution: float32 [4, 128, 256, 128], P(None, 'gx', 'gy')
All inputs are finite; a program needn't handle non-finite values.
Results may differ from a plain program's by a relative error of at most 0.0001.
Values sent between devices are 32-bit elements; how exact they have to be, the bound alone decides.
A program may use at most 320 MiB of HBM per device.

v0:
```python
import jax
import jax.numpy as jnp
from jax import lax
from jax.sharding import PartitionSpec as P

LEVELS = 6
SWEEPS = 2


def with_halo(block, sides, width):
    for axis, dim in sides:
        count = lax.axis_size(axis)
        forward = [(i, i + 1) for i in range(count - 1)]
        forward.append((count - 1, 0))
        backward = [(target, source) for source, target in forward]
        low = lax.ppermute(
            lax.slice_in_dim(block, block.shape[dim] - width, None, axis=dim), axis, forward
        )
        high = lax.ppermute(lax.slice_in_dim(block, 0, width, axis=dim), axis, backward)
        block = jnp.concatenate([low, block, high], axis=dim)
    return block


def restrict(field):
    k, a, b, c = field.shape
    blocks = field.reshape(k, a // 2, 2, b // 2, 2, c // 2, 2)
    return blocks.sum(axis=(2, 4, 6)) * 0.125


def prolong(field):
    return jnp.repeat(jnp.repeat(jnp.repeat(field, 2, axis=1), 2, axis=2), 2, axis=3)


def face_neighbours(field):
    padded = with_halo(field, (("gx", 1), ("gy", 2)), 1)
    total = padded[:, 2:, 1:-1] + padded[:, :-2, 1:-1]
    total = total + padded[:, 1:-1, 2:] + padded[:, 1:-1, :-2]
    total = total + jnp.roll(field, -1, 3) + jnp.roll(field, 1, 3)
    return total


def parity_mask(shape, start_x, start_y):
    full = (1, shape[1], shape[2], shape[3])
    ix = lax.broadcasted_iota(jnp.int32, full, 1) + start_x
    iy = lax.broadcasted_iota(jnp.int32, full, 2) + start_y
    iz = lax.broadcasted_iota(jnp.int32, full, 3)
    return (ix + iy + iz) % 2


def sweeps(field, source, coef, scale, parity, neighbours, from_zero):
    denom = coef + 6.0 * scale
    for sweep in range(SWEEPS):
        for colour in (0, 1):
            if from_zero and sweep == 0 and (colour == 0):
                field = jnp.where(parity == colour, source / denom, 0.0)
            else:
                fresh = (source + scale * neighbours(field)) / denom
                field = jnp.where(parity == colour, fresh, field)
    return field


def cycle(level, source, coef, neighbours, starts, descend):
    scale = 0.25**level
    parity = parity_mask(source.shape, starts[0], starts[1])
    field = sweeps(None, source, coef, scale, parity, neighbours, True)
    if level == LEVELS - 1:
        return field
    resid = source - (coef * field + scale * (6.0 * field - neighbours(field)))
    correction = descend(level + 1, restrict(resid))
    field = field + prolong(correction)
    return sweeps(field, source, coef, scale, parity, neighbours, False)


def local(rhs, coefficient):
    coefs = [coefficient]
    for level in range(LEVELS - 1):
        coefs.append(restrict(coefs[-1]))
    index_x = lax.axis_index("gx")
    index_y = lax.axis_index("gy")

    def starts_of(level):
        return (index_x * coefs[level].shape[1], index_y * coefs[level].shape[2])

    def descend(level, source):
        return cycle(level, source, coefs[level], face_neighbours, starts_of(level), descend)

    return descend(0, rhs)


def solution(mesh):
    in_specs = (P(None, "gx", "gy", None), P(None, "gx", "gy", None))
    out_specs = P(None, "gx", "gy", None)
    return jax.shard_map(local, mesh=mesh, in_specs=in_specs, out_specs=out_specs, check_vma=False)
```

profile of v0, /device:TPU:0, one launch (start us, length us, event | category | flops | bytes accessed | tf_op | source)
XLA Modules:
  0.0 1478.1 jit_solution(3230437389965576612)
XLA Ops:
  0.0 8.5 copy.1349
  8.5 7.5 copy.1215
  17.6 7.3 divide_select_fusion
  30.9 6.8 fusion.413
  37.7 32.9 %copy.1240 = f32[4,32,32,128]{0,3,2,1:T(8,128)} copy(f32[4,32,32,128]{3,2,1,0:T(8,128)} %param.3) | data formatting | bytes 4194304 | tf_op args[1]
  70.6 46.5 %reduce_sum.105 = f32[4,16,16,64]{0,3,2,1:T(8,128)} reduce(f32[4,16,2,16,2,64,2]{0,6,5,4,3,2,1:T(2,128)} %bitcast.1, f32[]{:T(128)} %constant.43.clone.1), dimensions={2,4,6}, to_apply=%region_1.0 | reduce | flops 458752 | bytes 2359300 | tf_op jit(solution)/shard_map/reduce_sum | solution.py:27
  131.8 8.2 fusion.390
  146.8 6.7 copy.1217
  169.4 36.3 %fusion.61 = f32[4,32,32,128]{2,1,3,0:T(8,128)} fusion(f32[4,32,32,128]{2,1,3,0:T(8,128)} %copy-done, f32[4,32,32,128]{2,1,3,0:T(8,128)} %copy.1349, f32[4,34,1,128]{2,1,3,0:T(8,128)} %copy.1220, f32[4,1,32,128]{2,1,3,0:T(1,128)S(1)} %collective-permute-done, f32[4,1,32,128]{2,1,3,0:T(1,128)S(1)} %collective-permute-done.1, f32[4,34,1,128]{2,1,3,0:T(8,128)} %copy.1218, ...), kind=kLoop, calls=%fused_computation.126 | loop fusion | flops 9961472 | bytes 12984320 | tf_op jit(solution)/shard_map/jit(_where)/select_n | solution.py:58
  212.1 12.8 fusion.410
  232.0 16.1 %fusion.389 = (f32[4,34,1,128]{2,1,3,0:T(8,128)}, f32[4,34,1,128]{2,1,3,0:T(8,128)}) fusion(f32[4,34,32,128]{2,1,3,0:T(8,128)} %pad_maximum_fusion.1), kind=kLoop, calls=%fused_computation.855 | loop fusion | bytes 278528 | tf_op jit(solution)/shard_map/slice | solution.py:19
  248.1 6.7 copy.1224
  254.8 6.7 copy.1222
  277.9 36.3 %fusion.53 = f32[4,32,32,128]{2,1,3,0:T(8,128)} fusion(f32[4,32,32,128]{2,1,3,0:T(8,128)} %fusion.61, f32[4,32,32,128]{2,1,3,0:T(8,128)} %copy.1349, f32[4,34,1,128]{2,1,3,0:T(8,128)} %copy.1225, f32[4,1,32,128]{2,1,3,0:T(1,128)S(1)} %collective-permute-done.4, f32[4,1,32,128]{2,1,3,0:T(1,128)S(1)} %collective-permute-done.5, f32[4,34,1,128]{2,1,3,0:T(8,128)} %copy.1223, ...), kind=kLoop, calls=%fused_computation.110 | loop fusion | flops 9961472 | bytes 12984320 | tf_op jit(solution)/shard_map/jit(_where)/select_n | solution.py:58
  318.9 11.5 fusion.407
  336.2 16.1 %fusion.388 = (f32[4,34,1,128]{2,1,3,0:T(8,128)}, f32[4,34,1,128]{2,1,3,0:T(8,128)}) fusion(f32[4,34,32,128]{2,1,3,0:T(8,128)} %pad_maximum_fusion.2), kind=kLoop, calls=%fused_computation.854 | loop fusion | bytes 278528 | tf_op jit(solution)/shard_map/slice | solution.py:19
  359.1 6.7 copy.1227
  382.4 36.2 %fusion.45 = f32[4,32,32,128]{2,1,3,0:T(8,128)} fusion(f32[4,32,32,128]{2,1,3,0:T(8,128)} %fusion.53, f32[4,32,32,128]{2,1,3,0:T(8,128)} %copy.1349, f32[4,34,1,128]{2,1,3,0:T(8,128)} %copy.1230, f32[4,1,32,128]{2,1,3,0:T(1,128)S(1)} %collective-permute-done.8, f32[4,1,32,128]{2,1,3,0:T(1,128)S(1)} %collective-permute-done.9, f32[4,34,1,128]{2,1,3,0:T(8,128)} %copy.1228, ...), kind=kLoop, calls=%fused_computation.94 | loop fusion | flops 9961472 | bytes 12984320 | tf_op jit(solution)/shard_map/jit(_where)/select_n | solution.py:58
  423.7 12.1 fusion.404
  441.7 16.1 %fusion.387 = (f32[4,34,1,128]{2,1,3,0:T(8,128)}, f32[4,34,1,128]{2,1,3,0:T(8,128)}) fusion(f32[4,34,32,128]{2,1,3,0:T(8,128)} %pad_maximum_fusion.3), kind=kLoop, calls=%fused_computation.853 | loop fusion | bytes 278528 | tf_op jit(solution)/shard_map/slice | solution.py:19
  457.8 6.7 copy.1235
  464.6 6.7 copy.1233
  487.6 39.7 %fusion.37 = f32[4,32,32,128]{2,1,3,0:T(8,128)} fusion(f32[4,32,32,128]{2,1,3,0:T(8,128)} %copy.1349, f32[4,34,1,128]{2,1,3,0:T(8,128)} %copy.1236, f32[4,1,32,128]{2,1,3,0:T(1,128)S(1)} %collective-permute-done.12, f32[4,32,32,128]{2,1,3,0:T(8,128)} %fusion.45, f32[4,1,32,128]{2,1,3,0:T(1,128)S(1)} %collective-permute-done.13, ...), kind=kLoop, calls=%fused_computation.78 | loop fusion | flops 10485760 | bytes 12853248 | tf_op jit(solution)/shard_map/sub | solution.py:68
  527.3 38.7 %copy.1238 = f32[4,32,32,128]{0,3,2,1:T(8,128)} copy(f32[4,32,32,128]{2,1,3,0:T(8,128)} %fusion.37) | data formatting | bytes 4194304 | tf_op jit(solution)/shard_map/sub | solution.py:68
  566.0 46.5 %reduce_sum.104 = f32[4,16,16,64]{0,3,2,1:T(8,128)} reduce(f32[4,16,2,16,2,64,2]{0,6,5,4,3,2,1:T(2,128)} %bitcast, f32[]{:T(128)} %constant.43.clone.1), dimensions={2,4,6}, to_apply=%region_0.0 | reduce | flops 458752 | bytes 2359300 | tf_op jit(solution)/shard_map/reduce_sum | solution.py:27
  634.8 9.0 reduce_sum.107
  686.0 9.0 reduce_sum.106
  1030.3 6.8 broadcast_in_dim.293
  1037.1 11.2 add.1394
  1053.0 11.3 fusion.401
  1070.2 16.1 %fusion.386 = (f32[4,34,1,128]{2,1,3,0:T(8,128)}, f32[4,34,1,128]{2,1,3,0:T(8,128)}) fusion(f32[4,34,32,128]{2,1,3,0:T(8,128)} %pad_maximum_fusion.4), kind=kLoop, calls=%fused_computation.852 | loop fusion | bytes 278528 | tf_op jit(solution)/shard_map/slice | solution.py:19
  1086.3 6.7 copy.1332
  1093.1 6.7 copy.1330
  1116.1 36.3 %fusion.29 = f32[4,32,32,128]{2,1,3,0:T(8,128)} fusion(f32[4,32,32,128]{2,1,3,0:T(8,128)} %add.1394, f32[4,32,32,128]{2,1,3,0:T(8,128)} %copy.1349, f32[4,34,1,128]{2,1,3,0:T(8,128)} %copy.1333, f32[4,1,32,128]{2,1,3,0:T(1,128)S(1)} %collective-permute-done.156, f32[4,1,32,128]{2,1,3,0:T(1,128)S(1)} %collective-permute-done.157, ...), kind=kLoop, calls=%fused_computation.62 | loop fusion | flops 9961472 | bytes 12984320 | tf_op jit(solution)/shard_map/jit(_where)/select_n | solution.py:58
  1157.7 11.5 fusion.398
  1175.1 16.1 %fusion.385 = (f32[4,34,1,128]{2,1,3,0:T(8,128)}, f32[4,34,1,128]{2,1,3,0:T(8,128)}) fusion(f32[4,34,32,128]{2,1,3,0:T(8,128)} %pad_maximum_fusion.5), kind=kLoop, calls=%fused_computation.851 | loop fusion | bytes 278528 | tf_op jit(solution)/shard_map/slice | solution.py:19
  1198.0 6.7 copy.1335
  1221.0 36.3 %fusion.21 = f32[4,32,32,128]{2,1,3,0:T(8,128)} fusion(f32[4,32,32,128]{2,1,3,0:T(8,128)} %fusion.29, f32[4,32,32,128]{2,1,3,0:T(8,128)} %copy.1349, f32[4,34,1,128]{2,1,3,0:T(8,128)} %copy.1338, f32[4,1,32,128]{2,1,3,0:T(1,128)S(1)} %collective-permute-done.160, f32[4,1,32,128]{2,1,3,0:T(1,128)S(1)} %collective-permute-done.161, ...), kind=kLoop, calls=%fused_computation.46 | loop fusion | flops 9961472 | bytes 12984320 | tf_op jit(solution)/shard_map/jit(_where)/select_n | solution.py:58
  1262.5 12.8 fusion.395
  1282.4 16.1 %fusion.384 = (f32[4,34,1,128]{2,1,3,0:T(8,128)}, f32[4,34,1,128]{2,1,3,0:T(8,128)}) fusion(f32[4,34,32,128]{2,1,3,0:T(8,128)} %pad_maximum_fusion.6), kind=kLoop, calls=%fused_computation.850 | loop fusion | bytes 278528 | tf_op jit(solution)/shard_map/slice | solution.py:19
  1298.5 6.7 copy.1342
  1305.2 6.7 copy.1340
  1328.5 36.2 %fusion.13 = f32[4,32,32,128]{2,1,3,0:T(8,128)} fusion(f32[4,32,32,128]{2,1,3,0:T(8,128)} %fusion.21, f32[4,32,32,128]{2,1,3,0:T(8,128)} %copy.1349, f32[4,34,1,128]{2,1,3,0:T(8,128)} %copy.1343, f32[4,1,32,128]{2,1,3,0:T(1,128)S(1)} %collective-permute-done.164, f32[4,1,32,128]{2,1,3,0:T(1,128)S(1)} %collective-permute-done.165, ...), kind=kLoop, calls=%fused_computation.30 | loop fusion | flops 9961472 | bytes 12984320 | tf_op jit(solution)/shard_map/jit(_where)/select_n | solution.py:58
  1369.4 12.5 fusion.392
  1388.3 16.1 %fusion.383 = (f32[4,34,1,128]{2,1,3,0:T(8,128)}, f32[4,34,1,128]{2,1,3,0:T(8,128)}) fusion(f32[4,34,32,128]{2,1,3,0:T(8,128)} %pad_maximum_fusion.7), kind=kLoop, calls=%fused_computation.849 | loop fusion | bytes 278528 | tf_op jit(solution)/shard_map/slice | solution.py:19
  1411.1 6.7 copy.1345
  1434.1 36.2 %fusion.5 = f32[4,32,32,128]{2,1,3,0:T(8,128)} fusion(f32[4,32,32,128]{2,1,3,0:T(8,128)} %fusion.13, f32[4,32,32,128]{2,1,3,0:T(8,128)} %copy.1349, f32[4,34,1,128]{2,1,3,0:T(8,128)} %copy.1348, f32[4,1,32,128]{2,1,3,0:T(1,128)S(1)} %collective-permute-done.168, f32[4,1,32,128]{2,1,3,0:T(1,128)S(1)} %collective-permute-done.169, ...), kind=kLoop, calls=%fused_computation.14 | loop fusion | flops 9961472 | bytes 12984320 | tf_op jit(solution)/shard_map/jit(_where)/select_n | solution.py:58
  1470.3 7.6 copy.1350
  (764 shorter events, 658.1 us)
Async XLA Ops:
  25.3 101.3 %collective-permute-start = (f32[4,1,32,128]{2,1,3,0:T(1,128)S(1)}, f32[4,1,32,128]{2,1,3,0:T(1,128)S(1)}, u32[]{:S(2)}, u32[]{:S(2)}) collective-permute-start(f32[4,1,32,128]{2,1,3,0:T(1,128)S(1)} %get-tuple-element.70), channel_id=1, source_target_pairs={{8,0},{16,8},{24,16},{0,24},{9,1},{17,9},{25,17},{1,25},{10,2},{18... | collective-permute-start | bytes 196616 | tf_op jit(solution)/shard_map/ppermute | solution.py:19
  30.4 96.2 %collective-permute-start.1 = (f32[4,1,32,128]{2,1,3,0:T(1,128)S(1)}, f32[4,1,32,128]{2,1,3,0:T(1,128)S(1)}, u32[]{:S(2)}, u32[]{:S(2)}) collective-permute-start(f32[4,1,32,128]{2,1,3,0:T(1,128)S(1)} %get-tuple-element.69), channel_id=1, source_target_pairs={{0,8},{8,16},{16,24},{24,0},{1,9},{9,17},{17,25},{25,1},{2,10},{10... | collective-permute-start | bytes 196616 | tf_op jit(solution)/shard_map/ppermute | solution.py:16
  146.7 10.1 collective-permute-start.3
  153.5 9.6 collective-permute-start.2
  208.2 16.7 %collective-permute-start.4 = (f32[4,1,32,128]{2,1,3,0:T(1,128)S(1)}, f32[4,1,32,128]{2,1,3,0:T(1,128)S(1)}, u32[]{:S(2)}, u32[]{:S(2)}) collective-permute-start(f32[4,1,32,128]{2,1,3,0:T(1,128)S(1)} %get-tuple-element.64), channel_id=1, source_target_pairs={{8,0},{16,8},{24,16},{0,24},{9,1},{17,9},{25,17},{1,25},{10,2},{18... | collective-permute-start | bytes 196616 | tf_op jit(solution)/shard_map/ppermute | solution.py:19
  212.1 12.8 collective-permute-start.5
  254.8 10.5 collective-permute-start.7
  261.6 10.1 collective-permute-start.6
  316.8 13.6 collective-permute-start.8
  317.5 12.9 collective-permute-start.9
  359.0 10.7 collective-permute-start.11
  365.8 10.3 collective-permute-start.10
  421.1 14.7 collective-permute-start.12
  423.0 12.9 collective-permute-start.13
  464.5 10.5 collective-permute-start.15
  471.3 10.0 collective-permute-start.14
  620.0 5.7 collective-permute-start.17
  625.8 18.6 %collective-permute-start.19 = (f32[4,18,1,64]{3,0,2,1:T(4,128)S(1)}, f32[4,18,1,64]{3,0,2,1:T(4,128)S(1)}, u32[]{:S(2)}, u32[]{:S(2)}) collective-permute-start(f32[4,18,1,64]{3,0,2,1:T(4,128)S(1)} %copy.1244), channel_id=1, source_target_pairs={{0,1},{1,2},{2,3},{3,4},{4,5},{5,6},{6,7},{7,0},{8,9},{9,10},{10,1... | collective-permute-start | bytes 55304 | tf_op jit(solution)/shard_map/ppermute | solution.py:16
  625.9 18.6 %collective-permute-start.18 = (f32[4,18,1,64]{3,0,2,1:T(4,128)S(1)}, f32[4,18,1,64]{3,0,2,1:T(4,128)S(1)}, u32[]{:S(2)}, u32[]{:S(2)}) collective-permute-start(f32[4,18,1,64]{3,0,2,1:T(4,128)S(1)} %copy.1242), channel_id=1, source_target_pairs={{1,0},{2,1},{3,2},{4,3},{5,4},{6,5},{7,6},{0,7},{9,8},{10,9},{11,1... | collective-permute-start | bytes 55304 | tf_op jit(solution)/shard_map/ppermute | solution.py:19
  647.7 5.7 collective-permute-start.21
  658.6 5.8 collective-permute-start.25
  669.8 5.7 collective-permute-start.29
  741.1 5.8 collective-permute-start.49
  751.8 5.7 collective-permute-start.53
  762.3 5.7 collective-permute-start.57
  773.0 5.7 collective-permute-start.61
  891.9 5.7 collective-permute-start.109
  913.2 5.7 collective-permute-start.117
  980.3 5.8 collective-permute-start.141
  991.4 5.7 collective-permute-start.145
  1002.4 5.7 collective-permute-start.149
  1013.5 5.7 collective-permute-start.153
  1050.9 13.5 collective-permute-start.156
  1051.0 13.4 collective-permute-start.157
  1093.0 10.5 collective-permute-start.159
  1099.8 10.0 collective-permute-start.158
  1155.0 14.3 collective-permute-start.160
  1156.4 12.9 collective-permute-start.161
  1197.9 10.6 collective-permute-start.163
  1204.7 10.1 collective-permute-start.162
  1259.9 15.4 %collective-permute-start.164 = (f32[4,1,32,128]{2,1,3,0:T(1,128)S(1)}, f32[4,1,32,128]{2,1,3,0:T(1,128)S(1)}, u32[]{:S(2)}, u32[]{:S(2)}) collective-permute-start(f32[4,1,32,128]{2,1,3,0:T(1,128)S(1)} %get-tuple-element.34), channel_id=1, source_target_pairs={{8,0},{16,8},{24,16},{0,24},{9,1},{17,9},{25,17},{1,25},{10,2},{18... | collective-permute-start | bytes 196616 | tf_op jit(solution)/shard_map/ppermute | solution.py:19
  1262.5 12.8 collective-permute-start.165
  1305.2 10.7 collective-permute-start.167
  1312.0 10.3 collective-permute-start.166
  1367.3 14.6 collective-permute-start.168
  1369.0 13.0 collective-permute-start.169
  1411.1 10.5 collective-permute-start.171
  1417.8 10.0 collective-permute-start.170
  (155 other events, 1892.7 us)
where the time goes:
time: 1490 us; the launch traced here: 1480 us
  local copies, waits for them, and re-layouts  596 us (40%)
  other arithmetic  487 us (33%)
  starting transfers between devices  215 us (14%)
  waiting for transfers between devices  177 us (12%)
    select_n x38, other arithmetic, sweeps(): field = jnp.where(parity == colour, fresh, field)  263 us
    slice x40, local copies, waits for them, and re-layouts, with_halo(): lax.slice_in_dim(block, 0, width, axis=dim)  175 us
    ppermute x86, starting transfers between devices, with_halo(): lax.ppermute(lax.slice_in_dim(block, 0, width, axis=dim), axis, backward)  141 us
    ppermute x86, waiting for transfers between devices, with_halo(): lax.ppermute(lax.slice_in_dim(block, block.shape[dim] - width, None, axis...  116 us
    reduce_sum x11, other arithmetic, restrict(): return blocks.sum(axis=(2, 4, 6)) * 0.125  113 us
    slice x86, local copies, waits for them, and re-layouts, face_neighbours(): total = total + jnp.roll(field, -1, 3) + jnp.roll(field, 1, 3)  105 us
    ppermute x86, starting transfers between devices, with_halo(): lax.ppermute(lax.slice_in_dim(block, block.shape[dim] - width, None, axis...  74 us
    slice x64, local copies, waits for them, and re-layouts, with_halo(): lax.slice_in_dim(block, block.shape[dim] - width, None, axis=dim)  72.4 us
  transfers between devices with their start and end apart: 172, of which 107 were waited for; matrix products, arithmetic and copies ran while one was open for 21% of the time, Pallas kernels for 0%

commit v1 on v0

v1 whole, which is shorter than its diff:
```python
import functools
import jax
import jax.numpy as jnp
import numpy as np
from jax import lax
from jax.experimental import pallas as pl
from jax.experimental.pallas import tpu as pltpu
from jax.sharding import PartitionSpec as P

LEVELS = 6
SPLIT = 3
W = 4
L = 128
VMEM = pl.BlockSpec(memory_space=pltpu.VMEM)


def iota(shape, dim):
    return lax.broadcasted_iota(jnp.int32, shape, dim)


def z_sum(v, group):
    axis = v.ndim - 1
    if group == L:
        return pltpu.roll(v, 1, axis) + pltpu.roll(v, L - 1, axis)
    place = iota(v.shape, axis) % group
    up = jnp.where(place == group - 1, pltpu.roll(v, group - 1, axis), pltpu.roll(v, L - 1, axis))
    down = jnp.where(place == 0, pltpu.roll(v, L - group + 1, axis), pltpu.roll(v, 1, axis))
    return up + down


def y_sum(v):
    axis, n = v.ndim - 2, v.shape[-2]
    return pltpu.roll(v, 1, axis) + pltpu.roll(v, n - 1, axis)


def squeeze_matrix(half, scale):
    source, target = iota((L, L), 0), iota((L, L), 1)
    return jnp.where(target == source // 2 + half * (L // 2), scale, 0.0).astype(jnp.float32)


def spread_matrix(half):
    source, target = iota((L, L), 0), iota((L, L), 1)
    return jnp.where(source == target // 2 + half * (L // 2), 1.0, 0.0).astype(jnp.float32)


def dot(a, b):
    return jnp.dot(a, b, preferred_element_type=jnp.float32, precision=lax.Precision.HIGHEST)


def fold(part, first, rows):
    count, nx = part.shape[0], part.shape[1]
    outs = []
    for a in range(0, count, 2):
        total = None
        for h in range(min(2, count - a)):
            m = squeeze_matrix(h, 0.125)
            even = jnp.concatenate([part[a + h, x, pl.ds(first, rows, stride=2), :] for x in range(nx)], 0)
            odd = jnp.concatenate([part[a + h, x, pl.ds(first + 1, rows, stride=2), :] for x in range(nx)], 0)
            term = dot(even + odd, m)
            total = term if total is None else total + term
        outs.append(total.reshape(nx, rows, L))
    return outs


def half_sweep(v, f_ref, w_ref, colour, low, high, group):
    count, rows = v.shape[0], v.shape[2]
    parity = (iota((rows, L), 0) + iota((rows, L), 1)) % 2

    def body(step, carry):
        for k in range(2):
            x = low + 2 * step + k
            mask = parity == (colour + low + k) % 2
            for c in range(count):
                mid = v[c, x]
                total = v[c, x - 1] + v[c, x + 1] + y_sum(mid) + z_sum(mid, group)
                v[c, x] = jnp.where(mask, f_ref[c, x] + w_ref[c, x] * total, mid)
        return carry

    lax.fori_loop(0, (high - low) // 2, body, 0)


def down_kernel(scale, group, f_in, c_in, f_out, w_out, v_out, g_out, v, part):
    count, nx, ny = v_out.shape[0], v_out.shape[1], v_out.shape[2]
    ex = f_in.shape[1]
    rows = f_in.shape[2]
    parity = (iota((rows, L), 0) + iota((rows, L), 1)) % 2

    def first(step, carry):
        for k in range(2):
            x = 2 * step + k
            for c in range(count):
                inverse = 1.0 / (c_in[c, x] + 6.0 * scale)
                fd = f_in[c, x] * inverse
                f_out[c, x] = fd
                w_out[c, x] = scale * inverse
                v[c, x] = jnp.where(parity == k, fd, 0.0)
        return carry

    lax.fori_loop(0, ex // 2, first, 0)
    half_sweep(v, f_out, w_out, 1, 1, ex - 1, group)
    half_sweep(v, f_out, w_out, 0, 2, ex - 2, group)
    half_sweep(v, f_out, w_out, 1, 3, ex - 3, group)

    def last(step, carry):
        for c in range(count):
            total = None
            for k in range(2):
                x = W + 2 * step + k
                mid = v[c, x]
                nb = v[c, x - 1] + v[c, x + 1] + y_sum(mid) + z_sum(mid, group)
                r = f_in[c, x] - (c_in[c, x] * mid + scale * (6.0 * mid - nb))
                v_out[c, 2 * step + k] = v[c, x, W : W + ny, :]
                total = r if total is None else total + r
            part[c, step] = total
        return carry

    lax.fori_loop(0, nx // 2, last, 0)
    for a, g in enumerate(fold(part, W, ny // 2)):
        g_out[a] = g


def spread(e, half, t):
    q = dot(e, spread_matrix(half))
    n = q.shape[0]
    t[pl.ds(0, n, stride=2), :] = q
    t[pl.ds(1, n, stride=2), :] = q


def post(v, f_ref, w_ref, group):
    ex = v.shape[1]
    for p, colour in ((1, 0), (2, 1), (3, 0), (4, 1)):
        half_sweep(v, f_ref, w_ref, colour, p, ex - p, group)


def up_kernel(scale, group, t_in, f_in, w_in, *rest):
    if len(rest) == 2:
        out, v = rest
        fine = None
    else:
        fine, out, v, t = rest
    ex = t_in.shape[1]

    def copy(x, carry):
        for c in range(t_in.shape[0]):
            v[c, x] = t_in[c, x]
        return carry

    lax.fori_loop(0, ex, copy, 0)
    finish(v, f_in, w_in, group, fine, out, None if fine is None else t)


def finish(v, f_in, w_in, group, fine, out, t):
    post(v, f_in, w_in, group)
    ex, ey = v.shape[1], v.shape[2]
    nx, ny = ex - 2 * W, ey - 2 * W
    if fine is None:

        def give(x, carry):
            for c in range(v.shape[0]):
                out[c, x] = v[c, W + x, W : W + ny, :]
            return carry

        lax.fori_loop(0, nx, give, 0)
        return
    for c in range(v.shape[0]):
        for h in range(2):
            q = dot(v[c, W : W + nx, W : W + ny, :].reshape(nx * ny, L), spread_matrix(h)).reshape(nx, ny, L)
            for x in range(nx):
                t[x, pl.ds(0, ny, stride=2), :] = q[x]
                t[x, pl.ds(1, ny, stride=2), :] = q[x]
            for x in range(nx):
                for k in range(2):
                    out[2 * c + h, 2 * x + k] = fine[2 * c + h, 2 * x + k] + t[x]


def up_last_kernel(scale, group, t_in, e_in, f_in, w_in, fine, out, v, te, t):
    for i in range(e_in.shape[0]):
        q = dot(e_in[i], spread_matrix(0))
        n = q.shape[0]
        te[i, pl.ds(0, n, stride=2), :] = q
        te[i, pl.ds(1, n, stride=2), :] = q
        for k in range(2):
            v[0, 2 * i + k] = t_in[0, 2 * i + k] + te[i]
    finish(v, f_in, w_in, group, fine, out, t)


def whole_neighbours(v, group):
    up = jnp.concatenate([v[1:], v[:1]], 0)
    down = jnp.concatenate([v[-1:], v[:-1]], 0)
    return up + down + y_sum(v) + z_sum(v, group)


def whole_cycle(level, f, coef, group, scratch):
    scale = 0.25**level
    inverse = 1.0 / (coef + 6.0 * scale)
    fd, w = f * inverse, scale * inverse
    parity = (iota(f.shape, 0) + iota(f.shape, 1) + iota(f.shape, 2)) % 2

    def sweep(v, colour):
        return jnp.where(parity == colour, fd + w * whole_neighbours(v, group), v)

    v = jnp.where(parity == 0, fd, 0.0)
    v = sweep(sweep(sweep(v, 1), 0), 1)
    if level == LEVELS - 1:
        return v
    part = scratch[0]
    nx, ny = f.shape[0], f.shape[1]

    def coarse(u):
        pairs = u.reshape(nx // 2, 2, ny, L)
        part[0] = pairs[:, 0] + pairs[:, 1]
        return fold(part, 0, ny // 2)[0]

    g = coarse(f - (coef * v + scale * (6.0 * v - whole_neighbours(v, group))))
    c = coarse(coef)
    e = whole_cycle(level + 1, g, c, group // 2, scratch[1:])
    q = dot(e.reshape(nx // 2 * (ny // 2), L), spread_matrix(0)).reshape(nx // 2, ny // 2, L)
    for x in range(nx // 2):
        part[0, x, pl.ds(0, ny // 2, stride=2), :] = q[x]
        part[0, x, pl.ds(1, ny // 2, stride=2), :] = q[x]
    t = part[0]
    v = v + jnp.concatenate([t[:, None], t[:, None]], 1).reshape(nx, ny, L)
    for colour in (0, 1, 0, 1):
        v = sweep(v, colour)
    return v


def whole_kernel(level, group, f_in, c_in, out, *scratch):
    out[...] = whole_cycle(level, f_in[...], c_in[...], group, scratch)


def coefs_kernel(c_in, *refs):
    outs, parts = refs[: len(refs) // 2], refs[len(refs) // 2 :]
    source = c_in
    for out, part in zip(outs, parts):
        for a in range(part.shape[0]):
            for x in range(part.shape[1]):
                part[a, x] = source[a, 2 * x] + source[a, 2 * x + 1]
        for a, g in enumerate(fold(part, 0, part.shape[2] // 2)):
            out[a] = g
        source = out


def call(kernel, inputs, outs, scratch):
    one = not isinstance(outs, list)
    shapes = [jax.ShapeDtypeStruct(s, jnp.float32) for s in ([outs] if one else outs)]
    result = pl.pallas_call(
        kernel,
        out_shape=shapes,
        in_specs=[VMEM] * len(inputs),
        out_specs=[VMEM] * len(shapes),
        scratch_shapes=[pltpu.VMEM(s, jnp.float32) for s in scratch],
        compiler_params=pltpu.CompilerParams(vmem_limit_bytes=48 * 1024 * 1024),
    )(*inputs)
    return result[0] if one else result


def shift(block, axis, step):
    count = lax.axis_size(axis)
    return lax.ppermute(block, axis, [(i, (i + step) % count) for i in range(count)])


def with_halo(arrays):
    counts = [a.shape[0] for a in arrays]

    def joined(cut):
        return jnp.concatenate([cut(a) for a in arrays], 0)

    x_low = shift(joined(lambda a: a[:, -W:]), "gx", 1)
    x_high = shift(joined(lambda a: a[:, :W]), "gx", -1)
    y_low = shift(joined(lambda a: a[:, :, -W:]), "gy", 1)
    y_high = shift(joined(lambda a: a[:, :, :W]), "gy", -1)
    sides = jnp.concatenate([y_low, y_high], 2)
    c_low = shift(sides[:, -W:], "gx", 1)
    c_high = shift(sides[:, :W], "gx", -1)
    results, at = [], 0
    for a, n in zip(arrays, counts):
        s = slice(at, at + n)
        at += n
        low = jnp.concatenate([c_low[s, :, :W], y_low[s], c_high[s, :, :W]], 1)
        high = jnp.concatenate([c_low[s, :, W:], y_high[s], c_high[s, :, W:]], 1)
        middle = jnp.concatenate([x_low[s], a, x_high[s]], 1)
        results.append(jnp.concatenate([low, middle, high], 2))
    return results


def gathered(own):
    whole = lax.all_gather(own[:, :, : L // 2], ("gx", "gy"))
    nx, ny = lax.axis_size("gx"), lax.axis_size("gy")
    whole = whole.reshape((nx, ny) + own.shape[:2] + (L // 2,)).transpose(0, 2, 1, 3, 4)
    whole = whole.reshape(nx * own.shape[0], ny * own.shape[1], L // 2)
    return jnp.pad(whole, ((0, 0), (0, 0), (0, L // 2)))


def local(rhs, coefficient):
    shapes = [rhs.shape]
    for _ in range(SPLIT):
        k, a, b, c = shapes[-1]
        shapes.append(((k + 1) // 2, a // 2, b // 2, L))

    def extended(shape):
        return (shape[0], shape[1] + 2 * W, shape[2] + 2 * W, L)

    coarser = call(
        coefs_kernel, [coefficient], shapes[1:],
        [(s[0], s[1] // 2, s[2], L) for s in shapes[:-1]],
    )
    coefs = [coefficient] + list(coarser)
    coef_whole = gathered(coefs[SPLIT][0])

    source = rhs
    fields, kept = [], []
    for level in range(SPLIT):
        shape = shapes[level]
        ext = extended(shape)
        if level == 0:
            f_ext, c_ext = with_halo([source, coefficient])
        else:
            (f_ext,) = with_halo([source])
            (c_ext,) = with_halo([coefs[level]])
        fd, w, v, source = call(
            functools.partial(down_kernel, 0.25**level, L >> level), [f_ext, c_ext],
            [ext, ext, shape, shapes[level + 1]],
            [ext, (shape[0], shape[1] // 2, ext[2], L)],
        )
        fields.append(v)
        kept.append((fd, w))

    group = L >> SPLIT
    f_whole = gathered(source[0])
    scratch = []
    nx, ny = f_whole.shape[0], f_whole.shape[1]
    for level in range(SPLIT, LEVELS - 1):
        scratch.append((1, nx // 2, ny, L))
        nx, ny = nx // 2, ny // 2
    e = call(functools.partial(whole_kernel, SPLIT, group), [f_whole, coef_whole], f_whole.shape, scratch)

    h = W // 2
    e = jnp.concatenate([e[-h:], e, e[:h]], 0)
    e = jnp.concatenate([e[:, -h:], e, e[:, :h]], 1)
    sx, sy = shapes[SPLIT][1], shapes[SPLIT][2]
    e = lax.dynamic_slice(
        e, (lax.axis_index("gx") * sx, lax.axis_index("gy") * sy, 0), (sx + 2 * h, sy + 2 * h, L)
    )
    level = SPLIT - 1
    (t_ext,) = with_halo([fields[level]])
    ext = extended(shapes[level])
    t = call(
        functools.partial(up_last_kernel, 0.25**level, L >> level),
        [t_ext, e, *kept[level], fields[level - 1]], shapes[level - 1],
        [ext, (sx + 2 * h, ext[2], L), (shapes[level][1], 2 * shapes[level][2], L)],
    )
    for level in range(SPLIT - 2, -1, -1):
        (t_ext,) = with_halo([t])
        inputs = [t_ext, *kept[level]]
        ext, shape = extended(shapes[level]), shapes[level]
        if level:
            t = call(
                functools.partial(up_kernel, 0.25**level, L >> level), inputs + [fields[level - 1]],
                shapes[level - 1], [ext, (shape[1], 2 * shape[2], L)],
            )
        else:
            t = call(functools.partial(up_kernel, 1.0, L), inputs, shape, [ext])
    return t


def solution(mesh):
    spec = P(None, "gx", "gy", None)
    return jax.shard_map(local, mesh=mesh, in_specs=(spec, spec), out_specs=spec, check_vma=False)
```

time: 1490 us -> 285 us (0.19)
  local copies, waits for them, and re-layouts: 596 us -> 9.47 us
  other arithmetic: 487 us -> 10.4 us
  starting transfers between devices: 215 us -> 61.3 us
  waiting for transfers between devices: 177 us -> 69 us
  blocking collectives: 0 us -> 80 us
  Pallas kernels: 0 us -> 53.9 us
    slice x190 -> x37, local copies, waits for them, and re-layouts: 353 us -> 7.55 us  [the longest x8 2.75 us: with_halo(): y_low = shift(joined(lambda a: a[:, :, -W:]), 'gy', 1)]
    select_n x41 -> x0, other arithmetic: 270 us -> none  [the longest x38 263 us: sweeps(): field = jnp.where(parity == colour, fresh, field)]
    ppermute x172 -> x48, starting transfers between devices: 215 us -> 61.3 us  [shift(): lax.ppermute(block, axis, [(i, (i + step) % count) for i in range(count)])]
    reduce_sum x11 -> x0, other arithmetic: 113 us -> none  [restrict(): return blocks.sum(axis=(2, 4, 6)) * 0.125]
    ppermute x172 -> x48, waiting for transfers between devices: 177 us -> 69 us  [shift(): lax.ppermute(block, axis, [(i, (i + step) % count) for i in range(count)])]
    ppermute x48 -> x0, local copies, waits for them, and re-layouts: 103 us -> none  [the longest x24 51.4 us: with_halo(): lax.ppermute(lax.slice_in_dim(block, block.shape[dim] - width, None, axis...]
    all_gather x0 -> x2, blocking collectives: none -> 80 us  [gathered(): whole = lax.all_gather(own[:, :, :L // 2], ('gx', 'gy'))]
    pallas_call x0 -> x8, Pallas kernels: none -> 53.9 us  [call(): pl.pallas_call(kernel, out_shape=shapes, in_specs=[VMEM] * len(inputs), o...]
  transfers between devices with their start and end apart: 172 -> 48, of which waited for: 107 -> 18; matrix products, arithmetic and copies ran while one was open for 21% -> 5% of each run, Pallas kernels for 0% -> 8%
where the time goes in v1:
time: 285 us
  blocking collectives  80 us (28%)
  waiting for transfers between devices  69 us (24%)
  starting transfers between devices  61.3 us (22%)
  Pallas kernels  53.9 us (19%)
  other arithmetic  10.4 us (4%)
  local copies, waits for them, and re-layouts  9.47 us (3%)
    all_gather x2, blocking collectives, gathered(): whole = lax.all_gather(own[:, :, :L // 2], ('gx', 'gy'))  80 us
    ppermute x48, waiting for transfers between devices, shift(): lax.ppermute(block, axis, [(i, (i + step) % count) for i in range(count)])  69 us
    ppermute x48, starting transfers between devices, shift(): lax.ppermute(block, axis, [(i, (i + step) % count) for i in range(count)])  61.3 us
    pallas_call x8, Pallas kernels, call(): pl.pallas_call(kernel, out_shape=shapes, in_specs=[VMEM] * len(inputs), o...  53.9 us
  transfers between devices with their start and end apart: 48, of which 18 were waited for; matrix products, arithmetic and copies ran while one was open for 5% of the time, Pallas kernels for 8%

profile of v1, /device:TPU:0, one launch (start us, length us, event | category | flops | bytes accessed | tf_op | source)
XLA Modules:
  0.0 284.7 jit_solution(17769908894162673787)
XLA Ops:
  0.0 1.9 fusion.15
  4.2 2.9 %collective-permute-start.1 = (f32[8,32,4,128]{3,2,1,0:T(4,128)}, f32[8,32,4,128]{3,2,1,0:T(4,128)}, u32[]{:S(2)}, u32[]{:S(2)}) collective-permute-start(f32[8,32,4,128]{3,2,1,0:T(4,128)} %pad_maximum_fusion.1), channel_id=1, source_target_pairs={{0,7},{1,0},{2,1},{3,2},{4,3},{5,4},{6,5},{7,6},{8,15},{9,8},{10,9... | collective-permute-start | bytes 1572872 | tf_op jit(solution)/shard_map/ppermute | solution.py:260
  9.0 2.3 collective-permute-start.4
  12.6 2.6 collective-permute-start.25
  18.7 1.6 collective-permute-start.26
  20.3 40.0 %all-gather.1 = f32[128,4,64]{2,1,0:T(4,128)S(1)} all-gather(f32[4,4,64]{2,1,0:T(4,128)S(1)} %bitcast.12), channel_id=3, replica_groups=mesh['gx'=4,'gy'=8] {'gx','gy'}, dimensions={0}, use_global_device_ids=true | all-gather | bytes 135168 | tf_op jit(solution)/shard_map/all_gather | solution.py:288
  60.5 2.1 collective-permute-done.13
  62.7 12.7 %collective-permute-done.27 = f32[1,4,8,128]{3,2,1,0:T(8,128)S(1)} collective-permute-done((f32[1,4,8,128]{3,2,1,0:T(8,128)}, f32[1,4,8,128]{3,2,1,0:T(8,128)S(1)}, u32[]{:S(2)}, u32[]{:S(2)}) %collective-permute-start.27) | collective-permute-done | bytes 16416 | tf_op jit(solution)/shard_map/ppermute | solution.py:260
  75.4 5.8 %collective-permute-done.14 = f32[2,4,8,128]{3,2,1,0:T(8,128)S(1)} collective-permute-done((f32[2,4,8,128]{3,2,1,0:T(8,128)S(1)}, f32[2,4,8,128]{3,2,1,0:T(8,128)S(1)}, u32[]{:S(2)}, u32[]{:S(2)}) %collective-permute-start.14) | collective-permute-done | bytes 32800 | tf_op jit(solution)/shard_map/ppermute | solution.py:260
  81.4 3.7 %collective-permute-done.15 = f32[2,4,8,128]{3,2,1,0:T(8,128)S(1)} collective-permute-done((f32[2,4,8,128]{3,2,1,0:T(8,128)S(1)}, f32[2,4,8,128]{3,2,1,0:T(8,128)S(1)}, u32[]{:S(2)}, u32[]{:S(2)}) %collective-permute-start.15) | collective-permute-done | bytes 32800 | tf_op jit(solution)/shard_map/ppermute | solution.py:260
  85.2 3.9 %collective-permute-start.17 = (f32[2,4,16,128]{3,2,1,0:T(8,128)}, f32[2,4,16,128]{3,2,1,0:T(8,128)S(1)}, u32[]{:S(2)}, u32[]{:S(2)}) collective-permute-start(f32[2,4,16,128]{3,2,1,0:T(8,128)} %get-tuple-element.66), channel_id=1, source_target_pairs={{0,24},{8,0},{16,8},{24,16},{1,25},{9,1},{17,9},{25,17},{2,26},{10... | collective-permute-start | bytes 196616 | tf_op jit(solution)/shard_map/ppermute | solution.py:260
  91.2 3.9 %collective-permute-start.29 = (f32[1,4,8,128]{3,2,1,0:T(8,128)S(1)}, f32[1,4,8,128]{3,2,1,0:T(8,128)S(1)}, u32[]{:S(2)}, u32[]{:S(2)}) collective-permute-start(f32[1,4,8,128]{3,2,1,0:T(8,128)S(1)} %copy-done.3), channel_id=1, source_target_pairs={{0,24},{8,0},{16,8},{24,16},{1,25},{9,1},{17,9},{25,17},{2,26},{10... | collective-permute-start | bytes 49160 | tf_op jit(solution)/shard_map/ppermute | solution.py:260
  96.2 6.8 %collective-permute-done.2 = f32[8,4,8,128]{3,2,1,0:T(8,128)S(1)} collective-permute-done((f32[8,4,8,128]{3,2,1,0:T(8,128)S(1)}, f32[8,4,8,128]{3,2,1,0:T(8,128)S(1)}, u32[]{:S(2)}, u32[]{:S(2)}) %collective-permute-start.2) | collective-permute-done | bytes 131104 | tf_op jit(solution)/shard_map/ppermute | solution.py:260
  103.0 4.9 %collective-permute-done.3 = f32[8,4,8,128]{3,2,1,0:T(8,128)S(1)} collective-permute-done((f32[8,4,8,128]{3,2,1,0:T(8,128)S(1)}, f32[8,4,8,128]{3,2,1,0:T(8,128)S(1)}, u32[]{:S(2)}, u32[]{:S(2)}) %collective-permute-start.3) | collective-permute-done | bytes 131104 | tf_op jit(solution)/shard_map/ppermute | solution.py:260
  108.0 2.1 maximum_maximum_fusion.1.c_in
  110.3 2.0 maximum_maximum_fusion.f_in
  112.2 16.4 %shard_map.28 = (f32[4,40,40,128]{3,2,1,0:T(8,128)S(1)}, f32[4,40,40,128]{3,2,1,0:T(8,128)}, f32[4,32,32,128]{3,2,1,0:T(8,128)S(1)}, f32[2,16,16,128]{3,2,1,0:T(8,128)S(1)}) custom-call(f32[4,40,40,128]{3,2,1,0:T(8,128)} %maximum_maximum_fusion.f_in, f32[4,40,40,128]{3,2,1,0:T(8,128)} %maximum_maximum_fusion.1.c_in), custom_call_target="tpu_custom_call" | custom-call | tf_op jit(solution)/shard_map/pallas_call | solution.py:247
  128.7 1.7 copy-done.1
  130.4 2.6 collective-permute-start.7
  133.1 1.8 collective-permute-done.6
  135.2 3.9 %collective-permute-start.11 = (f32[2,4,16,128]{3,2,1,0:T(8,128)S(1)}, f32[2,4,16,128]{3,2,1,0:T(8,128)S(1)}, u32[]{:S(2)}, u32[]{:S(2)}) collective-permute-start(f32[2,4,16,128]{3,2,1,0:T(8,128)S(1)} %get-tuple-element.70), channel_id=1, source_target_pairs={{0,24},{8,0},{16,8},{24,16},{1,25},{9,1},{17,9},{25,17},{2,26},{10... | collective-permute-start | bytes 196616 | tf_op jit(solution)/shard_map/ppermute | solution.py:260
  139.0 1.9 collective-permute-done.8
  141.0 3.8 %collective-permute-done.9 = f32[2,4,8,128]{3,2,1,0:T(8,128)S(1)} collective-permute-done((f32[2,4,8,128]{3,2,1,0:T(8,128)S(1)}, f32[2,4,8,128]{3,2,1,0:T(8,128)S(1)}, u32[]{:S(2)}, u32[]{:S(2)}) %collective-permute-start.9) | collective-permute-done | bytes 32800 | tf_op jit(solution)/shard_map/ppermute | solution.py:260
  144.9 5.2 %shard_map.30 = (f32[2,24,24,128]{3,2,1,0:T(8,128)S(1)}, f32[2,24,24,128]{3,2,1,0:T(8,128)S(1)}, f32[2,16,16,128]{3,2,1,0:T(8,128)S(1)}, f32[1,8,8,128]{3,2,1,0:T(8,128)S(1)}) custom-call(f32[2,24,24,128]{3,2,1,0:T(8,128)S(1)} %maximum_maximum_fusion.3.f_in, f32[2,24,24,128]{3,2,1,0:T(8,128)S(1)} %maximum_maximum_fusion.4.c_in), custom_call_target="tpu_custom_call" | custom-call | tf_op jit(solution)/shard_map/pallas_call | solution.py:247
  150.2 2.6 collective-permute-start.19
  154.4 3.8 %collective-permute-start.23 = (f32[1,4,8,128]{3,2,1,0:T(8,128)S(1)}, f32[1,4,8,128]{3,2,1,0:T(8,128)S(1)}, u32[]{:S(2)}, u32[]{:S(2)}) collective-permute-start(f32[1,4,8,128]{3,2,1,0:T(8,128)S(1)} %get-tuple-element.108), channel_id=1, source_target_pairs={{0,24},{8,0},{16,8},{24,16},{1,25},{9,1},{17,9},{25,17},{2,26},{10... | collective-permute-start | bytes 49160 | tf_op jit(solution)/shard_map/ppermute | solution.py:260
  158.2 2.0 collective-permute-start.21
  160.2 1.8 collective-permute-done.21
  162.0 2.3 shard_map.31
  164.3 40.0 %all-gather = f32[128,4,64]{2,1,0:T(4,128)S(1)} all-gather(f32[4,4,64]{2,1,0:T(4,128)S(1)} %bitcast.13), channel_id=2, replica_groups=mesh['gx'=4,'gy'=8] {'gx','gy'}, dimensions={0}, use_global_device_ids=true | all-gather | bytes 135168 | tf_op jit(solution)/shard_map/all_gather | solution.py:288
  204.4 4.7 %shard_map.32 = f32[16,32,128]{2,1,0:T(8,128)S(1)} custom-call(f32[16,32,128]{2,1,0:T(8,128)S(1)} %pad.7.f_in, f32[16,32,128]{2,1,0:T(8,128)S(1)} %pad.8.c_in), custom_call_target="tpu_custom_call" | custom-call | tf_op jit(solution)/shard_map/pallas_call | solution.py:247
  209.5 2.3 collective-permute-start.31
  211.8 3.8 %collective-permute-start.35 = (f32[1,4,8,128]{3,2,1,0:T(8,128)S(1)}, f32[1,4,8,128]{3,2,1,0:T(8,128)S(1)}, u32[]{:S(2)}, u32[]{:S(2)}) collective-permute-start(f32[1,4,8,128]{3,2,1,0:T(8,128)S(1)} %get-tuple-element.96), channel_id=1, source_target_pairs={{0,24},{8,0},{16,8},{24,16},{1,25},{9,1},{17,9},{25,17},{2,26},{10... | collective-permute-start | bytes 49160 | tf_op jit(solution)/shard_map/ppermute | solution.py:260
  215.9 3.8 %collective-permute-start.33 = (f32[1,4,8,128]{3,2,1,0:T(8,128)S(1)}, f32[1,4,8,128]{3,2,1,0:T(8,128)S(1)}, u32[]{:S(2)}, u32[]{:S(2)}) collective-permute-start(f32[1,4,8,128]{3,2,1,0:T(8,128)S(1)} %get-tuple-element.98), channel_id=1, source_target_pairs={{0,24},{8,0},{16,8},{24,16},{1,25},{9,1},{17,9},{25,17},{2,26},{10... | collective-permute-start | bytes 49160 | tf_op jit(solution)/shard_map/ppermute | solution.py:260
  219.7 1.5 collective-permute-done.32
  221.3 2.8 shard_map.33
  224.3 2.6 collective-permute-start.37
  226.9 1.9 collective-permute-done.36
  230.3 2.8 collective-permute-start.41
  233.0 2.0 collective-permute-start.39
  235.1 1.9 collective-permute-done.39
  237.1 5.5 %shard_map.34 = f32[4,32,32,128]{3,2,1,0:T(8,128)S(1)} custom-call(f32[2,24,24,128]{3,2,1,0:T(8,128)S(1)} %maximum_maximum_fusion.5.t_in, f32[2,24,24,128]{3,2,1,0:T(8,128)S(1)} %get-tuple-element.30.f_in, f32[2,24,24,128]{3,2,1,0:T(8,128)S(1)} %get-tuple-element.31.w_in, f32[4,32,32,128]{3,2,1,0:T(8,128)S(1)} %get-tuple-element.32.rest_0_), custom_call_target="tpu_custom_call" | custom-call | tf_op jit(solution)/shard_map/pallas_call | solution.py:247
  242.8 2.6 collective-permute-start.43
  245.4 6.4 %collective-permute-done.42 = f32[4,32,4,128]{3,2,1,0:T(4,128)S(1)} collective-permute-done((f32[4,32,4,128]{3,2,1,0:T(4,128)S(1)}, f32[4,32,4,128]{3,2,1,0:T(4,128)S(1)}, u32[]{:S(2)}, u32[]{:S(2)}) %collective-permute-start.42) | collective-permute-done | bytes 262176 | tf_op jit(solution)/shard_map/ppermute | solution.py:260
  251.8 1.9 collective-permute-start.44
  254.2 3.4 %collective-permute-start.47 = (f32[4,4,32,128]{3,2,1,0:T(8,128)S(1)}, f32[4,4,32,128]{3,2,1,0:T(8,128)S(1)}, u32[]{:S(2)}, u32[]{:S(2)}) collective-permute-start(f32[4,4,32,128]{3,2,1,0:T(8,128)S(1)} %get-tuple-element.36), channel_id=1, source_target_pairs={{0,24},{8,0},{16,8},{24,16},{1,25},{9,1},{17,9},{25,17},{2,26},{10... | collective-permute-start | bytes 786440 | tf_op jit(solution)/shard_map/ppermute | solution.py:260
  258.7 9.4 %collective-permute-done.45 = f32[4,4,8,128]{3,2,1,0:T(8,128)S(1)} collective-permute-done((f32[4,4,8,128]{3,2,1,0:T(8,128)S(1)}, f32[4,4,8,128]{3,2,1,0:T(8,128)S(1)}, u32[]{:S(2)}, u32[]{:S(2)}) %collective-permute-start.45) | collective-permute-done | bytes 65568 | tf_op jit(solution)/shard_map/ppermute | solution.py:260
  268.9 15.8 %shard_map.35 = f32[4,32,32,128]{3,2,1,0:T(8,128)} custom-call(f32[4,40,40,128]{3,2,1,0:T(8,128)S(1)} %maximum_maximum_fusion.2.t_in, f32[4,40,40,128]{3,2,1,0:T(8,128)} %copy-done.1, f32[4,40,40,128]{3,2,1,0:T(8,128)} %get-tuple-element.34.w_in), custom_call_target="tpu_custom_call" | custom-call | tf_op jit(solution)/shard_map/pallas_call | solution.py:247
  (129 shorter events, 19.7 us)
Async XLA Ops:
  2.8 82.3 %collective-permute-start = (f32[8,32,4,128]{3,2,1,0:T(4,128)}, f32[8,32,4,128]{3,2,1,0:T(4,128)S(1)}, u32[]{:S(2)}, u32[]{:S(2)}) collective-permute-start(f32[8,32,4,128]{3,2,1,0:T(4,128)} %pad_maximum_fusion), channel_id=1, source_target_pairs={{0,1},{1,2},{2,3},{3,4},{4,5},{5,6},{6,7},{7,0},{8,9},{9,10},{10,1... | collective-permute-start | bytes 1572872 | tf_op jit(solution)/shard_map/ppermute | solution.py:260
  4.2 84.8 %collective-permute-start.1 = (f32[8,32,4,128]{3,2,1,0:T(4,128)}, f32[8,32,4,128]{3,2,1,0:T(4,128)}, u32[]{:S(2)}, u32[]{:S(2)}) collective-permute-start(f32[8,32,4,128]{3,2,1,0:T(4,128)} %pad_maximum_fusion.1), channel_id=1, source_target_pairs={{0,7},{1,0},{2,1},{3,2},{4,3},{5,4},{6,5},{7,6},{8,15},{9,8},{10,9... | collective-permute-start | bytes 1572872 | tf_op jit(solution)/shard_map/ppermute | solution.py:260
  9.0 82.1 %collective-permute-start.4 = (f32[8,4,32,128]{3,2,1,0:T(8,128)}, f32[8,4,32,128]{3,2,1,0:T(8,128)}, u32[]{:S(2)}, u32[]{:S(2)}) collective-permute-start(f32[8,4,32,128]{3,2,1,0:T(8,128)} %pad_maximum_fusion.2), channel_id=1, source_target_pairs={{0,8},{8,16},{16,24},{24,0},{1,9},{9,17},{17,25},{25,1},{2,10},{10... | collective-permute-start | bytes 1572872 | tf_op jit(solution)/shard_map/ppermute | solution.py:260
  12.6 5.5 %collective-permute-start.24 = (f32[1,8,4,128]{3,2,1,0:T(4,128)S(1)}, f32[1,8,4,128]{3,2,1,0:T(4,128)S(1)}, u32[]{:S(2)}, u32[]{:S(2)}) collective-permute-start(f32[1,8,4,128]{3,2,1,0:T(4,128)S(1)} %get-tuple-element.105), channel_id=1, source_target_pairs={{0,1},{1,2},{2,3},{3,4},{4,5},{5,6},{6,7},{7,0},{8,9},{9,10},{10,1... | collective-permute-start | bytes 49160 | tf_op jit(solution)/shard_map/ppermute | solution.py:260
  12.6 5.5 %collective-permute-start.25 = (f32[1,8,4,128]{3,2,1,0:T(4,128)S(1)}, f32[1,8,4,128]{3,2,1,0:T(4,128)S(1)}, u32[]{:S(2)}, u32[]{:S(2)}) collective-permute-start(f32[1,8,4,128]{3,2,1,0:T(4,128)S(1)} %get-tuple-element.106), channel_id=1, source_target_pairs={{0,7},{1,0},{2,1},{3,2},{4,3},{5,4},{6,5},{7,6},{8,15},{9,8},{10,9... | collective-permute-start | bytes 49160 | tf_op jit(solution)/shard_map/ppermute | solution.py:260
  18.0 42.4 %collective-permute-start.12 = (f32[2,16,4,128]{3,2,1,0:T(4,128)}, f32[2,16,4,128]{3,2,1,0:T(4,128)S(1)}, u32[]{:S(2)}, u32[]{:S(2)}) collective-permute-start(f32[2,16,4,128]{3,2,1,0:T(4,128)} %get-tuple-element.67), channel_id=1, source_target_pairs={{0,1},{1,2},{2,3},{3,4},{4,5},{5,6},{6,7},{7,0},{8,9},{9,10},{10,1... | collective-permute-start | bytes 196616 | tf_op jit(solution)/shard_map/ppermute | solution.py:260
  18.7 41.7 %collective-permute-start.26 = (f32[1,4,8,128]{3,2,1,0:T(8,128)}, f32[1,4,8,128]{3,2,1,0:T(8,128)S(1)}, u32[]{:S(2)}, u32[]{:S(2)}) collective-permute-start(f32[1,4,8,128]{3,2,1,0:T(8,128)} %get-tuple-element.103), channel_id=1, source_target_pairs={{0,8},{8,16},{16,24},{24,0},{1,9},{9,17},{17,25},{25,1},{2,10},{10... | collective-permute-start | bytes 49160 | tf_op jit(solution)/shard_map/ppermute | solution.py:260
  60.4 2.3 collective-permute-start.13
  60.5 35.6 %collective-permute-start.5 = (f32[8,4,32,128]{3,2,1,0:T(8,128)}, f32[8,4,32,128]{3,2,1,0:T(8,128)S(1)}, u32[]{:S(2)}, u32[]{:S(2)}) collective-permute-start(f32[8,4,32,128]{3,2,1,0:T(8,128)} %pad_maximum_fusion.3), channel_id=1, source_target_pairs={{0,24},{8,0},{16,8},{24,16},{1,25},{9,1},{17,9},{25,17},{2,26},{10... | collective-permute-start | bytes 1572872 | tf_op jit(solution)/shard_map/ppermute | solution.py:260
  62.7 12.7 %collective-permute-start.27 = (f32[1,4,8,128]{3,2,1,0:T(8,128)}, f32[1,4,8,128]{3,2,1,0:T(8,128)S(1)}, u32[]{:S(2)}, u32[]{:S(2)}) collective-permute-start(f32[1,4,8,128]{3,2,1,0:T(8,128)} %get-tuple-element.104), channel_id=1, source_target_pairs={{0,24},{8,0},{16,8},{24,16},{1,25},{9,1},{17,9},{25,17},{2,26},{10... | collective-permute-start | bytes 49160 | tf_op jit(solution)/shard_map/ppermute | solution.py:260
  75.4 5.8 %collective-permute-start.14 = (f32[2,4,8,128]{3,2,1,0:T(8,128)S(1)}, f32[2,4,8,128]{3,2,1,0:T(8,128)S(1)}, u32[]{:S(2)}, u32[]{:S(2)}) collective-permute-start(f32[2,4,8,128]{3,2,1,0:T(8,128)S(1)} %get-tuple-element.75), channel_id=1, source_target_pairs={{0,8},{8,16},{16,24},{24,0},{1,9},{9,17},{17,25},{25,1},{2,10},{10... | collective-permute-start | bytes 98312 | tf_op jit(solution)/shard_map/ppermute | solution.py:260
  81.2 3.9 %collective-permute-start.15 = (f32[2,4,8,128]{3,2,1,0:T(8,128)S(1)}, f32[2,4,8,128]{3,2,1,0:T(8,128)S(1)}, u32[]{:S(2)}, u32[]{:S(2)}) collective-permute-start(f32[2,4,8,128]{3,2,1,0:T(8,128)S(1)} %get-tuple-element.76), channel_id=1, source_target_pairs={{0,24},{8,0},{16,8},{24,16},{1,25},{9,1},{17,9},{25,17},{2,26},{10... | collective-permute-start | bytes 98312 | tf_op jit(solution)/shard_map/ppermute | solution.py:260
  85.1 45.3 %collective-permute-start.16 = (f32[2,4,16,128]{3,2,1,0:T(8,128)}, f32[2,4,16,128]{3,2,1,0:T(8,128)S(1)}, u32[]{:S(2)}, u32[]{:S(2)}) collective-permute-start(f32[2,4,16,128]{3,2,1,0:T(8,128)} %get-tuple-element.65), channel_id=1, source_target_pairs={{0,8},{8,16},{16,24},{24,0},{1,9},{9,17},{17,25},{25,1},{2,10},{10... | collective-permute-start | bytes 196616 | tf_op jit(solution)/shard_map/ppermute | solution.py:260
  85.2 47.9 %collective-permute-start.17 = (f32[2,4,16,128]{3,2,1,0:T(8,128)}, f32[2,4,16,128]{3,2,1,0:T(8,128)S(1)}, u32[]{:S(2)}, u32[]{:S(2)}) collective-permute-start(f32[2,4,16,128]{3,2,1,0:T(8,128)} %get-tuple-element.66), channel_id=1, source_target_pairs={{0,24},{8,0},{16,8},{24,16},{1,25},{9,1},{17,9},{25,17},{2,26},{10... | collective-permute-start | bytes 196616 | tf_op jit(solution)/shard_map/ppermute | solution.py:260
  89.1 63.7 %collective-permute-start.28 = (f32[1,4,8,128]{3,2,1,0:T(8,128)}, f32[1,4,8,128]{3,2,1,0:T(8,128)S(1)}, u32[]{:S(2)}, u32[]{:S(2)}) collective-permute-start(f32[1,4,8,128]{3,2,1,0:T(8,128)} %get-tuple-element.101), channel_id=1, source_target_pairs={{0,8},{8,16},{16,24},{24,0},{1,9},{9,17},{17,25},{25,1},{2,10},{10... | collective-permute-start | bytes 49160 | tf_op jit(solution)/shard_map/ppermute | solution.py:260
  91.2 61.7 %collective-permute-start.29 = (f32[1,4,8,128]{3,2,1,0:T(8,128)S(1)}, f32[1,4,8,128]{3,2,1,0:T(8,128)S(1)}, u32[]{:S(2)}, u32[]{:S(2)}) collective-permute-start(f32[1,4,8,128]{3,2,1,0:T(8,128)S(1)} %copy-done.3), channel_id=1, source_target_pairs={{0,24},{8,0},{16,8},{24,16},{1,25},{9,1},{17,9},{25,17},{2,26},{10... | collective-permute-start | bytes 49160 | tf_op jit(solution)/shard_map/ppermute | solution.py:260
  96.1 6.9 %collective-permute-start.2 = (f32[8,4,8,128]{3,2,1,0:T(8,128)S(1)}, f32[8,4,8,128]{3,2,1,0:T(8,128)S(1)}, u32[]{:S(2)}, u32[]{:S(2)}) collective-permute-start(f32[8,4,8,128]{3,2,1,0:T(8,128)S(1)} %get-tuple-element.47), channel_id=1, source_target_pairs={{0,8},{8,16},{16,24},{24,0},{1,9},{9,17},{17,25},{25,1},{2,10},{10... | collective-permute-start | bytes 393224 | tf_op jit(solution)/shard_map/ppermute | solution.py:260
  103.0 5.0 %collective-permute-start.3 = (f32[8,4,8,128]{3,2,1,0:T(8,128)S(1)}, f32[8,4,8,128]{3,2,1,0:T(8,128)S(1)}, u32[]{:S(2)}, u32[]{:S(2)}) collective-permute-start(f32[8,4,8,128]{3,2,1,0:T(8,128)S(1)} %get-tuple-element.48), channel_id=1, source_target_pairs={{0,24},{8,0},{16,8},{24,16},{1,25},{9,1},{17,9},{25,17},{2,26},{10... | collective-permute-start | bytes 393224 | tf_op jit(solution)/shard_map/ppermute | solution.py:260
  130.3 4.6 %collective-permute-start.6 = (f32[2,16,4,128]{3,2,1,0:T(4,128)S(1)}, f32[2,16,4,128]{3,2,1,0:T(4,128)S(1)}, u32[]{:S(2)}, u32[]{:S(2)}) collective-permute-start(f32[2,16,4,128]{3,2,1,0:T(4,128)S(1)} %get-tuple-element.71), channel_id=1, source_target_pairs={{0,1},{1,2},{2,3},{3,4},{4,5},{5,6},{6,7},{7,0},{8,9},{9,10},{10,1... | collective-permute-start | bytes 196616 | tf_op jit(solution)/shard_map/ppermute | solution.py:260
  130.4 4.6 %collective-permute-start.7 = (f32[2,16,4,128]{3,2,1,0:T(4,128)S(1)}, f32[2,16,4,128]{3,2,1,0:T(4,128)S(1)}, u32[]{:S(2)}, u32[]{:S(2)}) collective-permute-start(f32[2,16,4,128]{3,2,1,0:T(4,128)S(1)} %get-tuple-element.72), channel_id=1, source_target_pairs={{0,7},{1,0},{2,1},{3,2},{4,3},{5,4},{6,5},{7,6},{8,15},{9,8},{10,9... | collective-permute-start | bytes 196616 | tf_op jit(solution)/shard_map/ppermute | solution.py:260
  135.0 5.9 %collective-permute-start.8 = (f32[2,4,8,128]{3,2,1,0:T(8,128)S(1)}, f32[2,4,8,128]{3,2,1,0:T(8,128)S(1)}, u32[]{:S(2)}, u32[]{:S(2)}) collective-permute-start(f32[2,4,8,128]{3,2,1,0:T(8,128)S(1)} %get-tuple-element.77), channel_id=1, source_target_pairs={{0,8},{8,16},{16,24},{24,0},{1,9},{9,17},{17,25},{25,1},{2,10},{10... | collective-permute-start | bytes 98312 | tf_op jit(solution)/shard_map/ppermute | solution.py:260
  135.1 9.7 %collective-permute-start.10 = (f32[2,4,16,128]{3,2,1,0:T(8,128)S(1)}, f32[2,4,16,128]{3,2,1,0:T(8,128)S(1)}, u32[]{:S(2)}, u32[]{:S(2)}) collective-permute-start(f32[2,4,16,128]{3,2,1,0:T(8,128)S(1)} %get-tuple-element.69), channel_id=1, source_target_pairs={{0,8},{8,16},{16,24},{24,0},{1,9},{9,17},{17,25},{25,1},{2,10},{10... | collective-permute-start | bytes 196616 | tf_op jit(solution)/shard_map/ppermute | solution.py:260
  135.2 9.6 %collective-permute-start.11 = (f32[2,4,16,128]{3,2,1,0:T(8,128)S(1)}, f32[2,4,16,128]{3,2,1,0:T(8,128)S(1)}, u32[]{:S(2)}, u32[]{:S(2)}) collective-permute-start(f32[2,4,16,128]{3,2,1,0:T(8,128)S(1)} %get-tuple-element.70), channel_id=1, source_target_pairs={{0,24},{8,0},{16,8},{24,16},{1,25},{9,1},{17,9},{25,17},{2,26},{10... | collective-permute-start | bytes 196616 | tf_op jit(solution)/shard_map/ppermute | solution.py:260
  140.9 3.9 %collective-permute-start.9 = (f32[2,4,8,128]{3,2,1,0:T(8,128)S(1)}, f32[2,4,8,128]{3,2,1,0:T(8,128)S(1)}, u32[]{:S(2)}, u32[]{:S(2)}) collective-permute-start(f32[2,4,8,128]{3,2,1,0:T(8,128)S(1)} %get-tuple-element.78), channel_id=1, source_target_pairs={{0,24},{8,0},{16,8},{24,16},{1,25},{9,1},{17,9},{25,17},{2,26},{10... | collective-permute-start | bytes 98312 | tf_op jit(solution)/shard_map/ppermute | solution.py:260
  150.1 4.1 %collective-permute-start.18 = (f32[1,8,4,128]{3,2,1,0:T(4,128)S(1)}, f32[1,8,4,128]{3,2,1,0:T(4,128)S(1)}, u32[]{:S(2)}, u32[]{:S(2)}) collective-permute-start(f32[1,8,4,128]{3,2,1,0:T(4,128)S(1)} %get-tuple-element.111), channel_id=1, source_target_pairs={{0,1},{1,2},{2,3},{3,4},{4,5},{5,6},{6,7},{7,0},{8,9},{9,10},{10,1... | collective-permute-start | bytes 49160 | tf_op jit(solution)/shard_map/ppermute | solution.py:260
  150.2 4.1 %collective-permute-start.19 = (f32[1,8,4,128]{3,2,1,0:T(4,128)S(1)}, f32[1,8,4,128]{3,2,1,0:T(4,128)S(1)}, u32[]{:S(2)}, u32[]{:S(2)}) collective-permute-start(f32[1,8,4,128]{3,2,1,0:T(4,128)S(1)} %get-tuple-element.112), channel_id=1, source_target_pairs={{0,7},{1,0},{2,1},{3,2},{4,3},{5,4},{6,5},{7,6},{8,15},{9,8},{10,9... | collective-permute-start | bytes 49160 | tf_op jit(solution)/shard_map/ppermute | solution.py:260
  154.3 5.9 %collective-permute-start.20 = (f32[1,4,8,128]{3,2,1,0:T(8,128)S(1)}, f32[1,4,8,128]{3,2,1,0:T(8,128)S(1)}, u32[]{:S(2)}, u32[]{:S(2)}) collective-permute-start(f32[1,4,8,128]{3,2,1,0:T(8,128)S(1)} %get-tuple-element.109), channel_id=1, source_target_pairs={{0,8},{8,16},{16,24},{24,0},{1,9},{9,17},{17,25},{25,1},{2,10},{10... | collective-permute-start | bytes 49160 | tf_op jit(solution)/shard_map/ppermute | solution.py:260
  154.3 7.6 %collective-permute-start.22 = (f32[1,4,8,128]{3,2,1,0:T(8,128)S(1)}, f32[1,4,8,128]{3,2,1,0:T(8,128)S(1)}, u32[]{:S(2)}, u32[]{:S(2)}) collective-permute-start(f32[1,4,8,128]{3,2,1,0:T(8,128)S(1)} %get-tuple-element.107), channel_id=1, source_target_pairs={{0,8},{8,16},{16,24},{24,0},{1,9},{9,17},{17,25},{25,1},{2,10},{10... | collective-permute-start | bytes 49160 | tf_op jit(solution)/shard_map/ppermute | solution.py:260
  154.4 7.6 %collective-permute-start.23 = (f32[1,4,8,128]{3,2,1,0:T(8,128)S(1)}, f32[1,4,8,128]{3,2,1,0:T(8,128)S(1)}, u32[]{:S(2)}, u32[]{:S(2)}) collective-permute-start(f32[1,4,8,128]{3,2,1,0:T(8,128)S(1)} %get-tuple-element.108), channel_id=1, source_target_pairs={{0,24},{8,0},{16,8},{24,16},{1,25},{9,1},{17,9},{25,17},{2,26},{10... | collective-permute-start | bytes 49160 | tf_op jit(solution)/shard_map/ppermute | solution.py:260
  158.2 3.7 %collective-permute-start.21 = (f32[1,4,8,128]{3,2,1,0:T(8,128)S(1)}, f32[1,4,8,128]{3,2,1,0:T(8,128)S(1)}, u32[]{:S(2)}, u32[]{:S(2)}) collective-permute-start(f32[1,4,8,128]{3,2,1,0:T(8,128)S(1)} %get-tuple-element.110), channel_id=1, source_target_pairs={{0,24},{8,0},{16,8},{24,16},{1,25},{9,1},{17,9},{25,17},{2,26},{10... | collective-permute-start | bytes 49160 | tf_op jit(solution)/shard_map/ppermute | solution.py:260
  209.1 6.5 %collective-permute-start.30 = (f32[1,8,4,128]{3,2,1,0:T(4,128)S(1)}, f32[1,8,4,128]{3,2,1,0:T(4,128)S(1)}, u32[]{:S(2)}, u32[]{:S(2)}) collective-permute-start(f32[1,8,4,128]{3,2,1,0:T(4,128)S(1)} %get-tuple-element.99), channel_id=1, source_target_pairs={{0,1},{1,2},{2,3},{3,4},{4,5},{5,6},{6,7},{7,0},{8,9},{9,10},{10,1... | collective-permute-start | bytes 49160 | tf_op jit(solution)/shard_map/ppermute | solution.py:260
  209.5 6.1 %collective-permute-start.31 = (f32[1,8,4,128]{3,2,1,0:T(4,128)S(1)}, f32[1,8,4,128]{3,2,1,0:T(4,128)S(1)}, u32[]{:S(2)}, u32[]{:S(2)}) collective-permute-start(f32[1,8,4,128]{3,2,1,0:T(4,128)S(1)} %get-tuple-element.100), channel_id=1, source_target_pairs={{0,7},{1,0},{2,1},{3,2},{4,3},{5,4},{6,5},{7,6},{8,15},{9,8},{10,9... | collective-permute-start | bytes 49160 | tf_op jit(solution)/shard_map/ppermute | solution.py:260
  211.8 9.5 %collective-permute-start.34 = (f32[1,4,8,128]{3,2,1,0:T(8,128)S(1)}, f32[1,4,8,128]{3,2,1,0:T(8,128)S(1)}, u32[]{:S(2)}, u32[]{:S(2)}) collective-permute-start(f32[1,4,8,128]{3,2,1,0:T(8,128)S(1)} %get-tuple-element.95), channel_id=1, source_target_pairs={{0,8},{8,16},{16,24},{24,0},{1,9},{9,17},{17,25},{25,1},{2,10},{10... | collective-permute-start | bytes 49160 | tf_op jit(solution)/shard_map/ppermute | solution.py:260
  211.8 9.5 %collective-permute-start.35 = (f32[1,4,8,128]{3,2,1,0:T(8,128)S(1)}, f32[1,4,8,128]{3,2,1,0:T(8,128)S(1)}, u32[]{:S(2)}, u32[]{:S(2)}) collective-permute-start(f32[1,4,8,128]{3,2,1,0:T(8,128)S(1)} %get-tuple-element.96), channel_id=1, source_target_pairs={{0,24},{8,0},{16,8},{24,16},{1,25},{9,1},{17,9},{25,17},{2,26},{10... | collective-permute-start | bytes 49160 | tf_op jit(solution)/shard_map/ppermute | solution.py:260
  215.7 5.6 %collective-permute-start.32 = (f32[1,4,8,128]{3,2,1,0:T(8,128)S(1)}, f32[1,4,8,128]{3,2,1,0:T(8,128)S(1)}, u32[]{:S(2)}, u32[]{:S(2)}) collective-permute-start(f32[1,4,8,128]{3,2,1,0:T(8,128)S(1)} %get-tuple-element.97), channel_id=1, source_target_pairs={{0,8},{8,16},{16,24},{24,0},{1,9},{9,17},{17,25},{25,1},{2,10},{10... | collective-permute-start | bytes 49160 | tf_op jit(solution)/shard_map/ppermute | solution.py:260
  215.9 5.4 %collective-permute-start.33 = (f32[1,4,8,128]{3,2,1,0:T(8,128)S(1)}, f32[1,4,8,128]{3,2,1,0:T(8,128)S(1)}, u32[]{:S(2)}, u32[]{:S(2)}) collective-permute-start(f32[1,4,8,128]{3,2,1,0:T(8,128)S(1)} %get-tuple-element.98), channel_id=1, source_target_pairs={{0,24},{8,0},{16,8},{24,16},{1,25},{9,1},{17,9},{25,17},{2,26},{10... | collective-permute-start | bytes 49160 | tf_op jit(solution)/shard_map/ppermute | solution.py:260
  224.2 4.6 %collective-permute-start.36 = (f32[2,16,4,128]{3,2,1,0:T(4,128)S(1)}, f32[2,16,4,128]{3,2,1,0:T(4,128)S(1)}, u32[]{:S(2)}, u32[]{:S(2)}) collective-permute-start(f32[2,16,4,128]{3,2,1,0:T(4,128)S(1)} %get-tuple-element.61), channel_id=1, source_target_pairs={{0,1},{1,2},{2,3},{3,4},{4,5},{5,6},{6,7},{7,0},{8,9},{9,10},{10,1... | collective-permute-start | bytes 196616 | tf_op jit(solution)/shard_map/ppermute | solution.py:260
  224.3 4.6 %collective-permute-start.37 = (f32[2,16,4,128]{3,2,1,0:T(4,128)S(1)}, f32[2,16,4,128]{3,2,1,0:T(4,128)S(1)}, u32[]{:S(2)}, u32[]{:S(2)}) collective-permute-start(f32[2,16,4,128]{3,2,1,0:T(4,128)S(1)} %get-tuple-element.62), channel_id=1, source_target_pairs={{0,7},{1,0},{2,1},{3,2},{4,3},{5,4},{6,5},{7,6},{8,15},{9,8},{10,9... | collective-permute-start | bytes 196616 | tf_op jit(solution)/shard_map/ppermute | solution.py:260
  228.9 6.2 %collective-permute-start.38 = (f32[2,4,8,128]{3,2,1,0:T(8,128)S(1)}, f32[2,4,8,128]{3,2,1,0:T(8,128)S(1)}, u32[]{:S(2)}, u32[]{:S(2)}) collective-permute-start(f32[2,4,8,128]{3,2,1,0:T(8,128)S(1)} %get-tuple-element.73), channel_id=1, source_target_pairs={{0,8},{8,16},{16,24},{24,0},{1,9},{9,17},{17,25},{25,1},{2,10},{10... | collective-permute-start | bytes 98312 | tf_op jit(solution)/shard_map/ppermute | solution.py:260
  228.9 8.0 %collective-permute-start.40 = (f32[2,4,16,128]{3,2,1,0:T(8,128)S(1)}, f32[2,4,16,128]{3,2,1,0:T(8,128)S(1)}, u32[]{:S(2)}, u32[]{:S(2)}) collective-permute-start(f32[2,4,16,128]{3,2,1,0:T(8,128)S(1)} %get-tuple-element.59), channel_id=1, source_target_pairs={{0,8},{8,16},{16,24},{24,0},{1,9},{9,17},{17,25},{25,1},{2,10},{10... | collective-permute-start | bytes 196616 | tf_op jit(solution)/shard_map/ppermute | solution.py:260
  230.3 6.7 %collective-permute-start.41 = (f32[2,4,16,128]{3,2,1,0:T(8,128)S(1)}, f32[2,4,16,128]{3,2,1,0:T(8,128)S(1)}, u32[]{:S(2)}, u32[]{:S(2)}) collective-permute-start(f32[2,4,16,128]{3,2,1,0:T(8,128)S(1)} %get-tuple-element.60), channel_id=1, source_target_pairs={{0,24},{8,0},{16,8},{24,16},{1,25},{9,1},{17,9},{25,17},{2,26},{10... | collective-permute-start | bytes 196616 | tf_op jit(solution)/shard_map/ppermute | solution.py:260
  233.0 3.9 %collective-permute-start.39 = (f32[2,4,8,128]{3,2,1,0:T(8,128)S(1)}, f32[2,4,8,128]{3,2,1,0:T(8,128)S(1)}, u32[]{:S(2)}, u32[]{:S(2)}) collective-permute-start(f32[2,4,8,128]{3,2,1,0:T(8,128)S(1)} %get-tuple-element.74), channel_id=1, source_target_pairs={{0,24},{8,0},{16,8},{24,16},{1,25},{9,1},{17,9},{25,17},{2,26},{10... | collective-permute-start | bytes 98312 | tf_op jit(solution)/shard_map/ppermute | solution.py:260
  242.7 9.1 %collective-permute-start.42 = (f32[4,32,4,128]{3,2,1,0:T(4,128)S(1)}, f32[4,32,4,128]{3,2,1,0:T(4,128)S(1)}, u32[]{:S(2)}, u32[]{:S(2)}) collective-permute-start(f32[4,32,4,128]{3,2,1,0:T(4,128)S(1)} %get-tuple-element.37), channel_id=1, source_target_pairs={{0,1},{1,2},{2,3},{3,4},{4,5},{5,6},{6,7},{7,0},{8,9},{9,10},{10,1... | collective-permute-start | bytes 786440 | tf_op jit(solution)/shard_map/ppermute | solution.py:260
  242.8 9.0 %collective-permute-start.43 = (f32[4,32,4,128]{3,2,1,0:T(4,128)S(1)}, f32[4,32,4,128]{3,2,1,0:T(4,128)S(1)}, u32[]{:S(2)}, u32[]{:S(2)}) collective-permute-start(f32[4,32,4,128]{3,2,1,0:T(4,128)S(1)} %get-tuple-element.38), channel_id=1, source_target_pairs={{0,7},{1,0},{2,1},{3,2},{4,3},{5,4},{6,5},{7,6},{8,15},{9,8},{10,9... | collective-permute-start | bytes 786440 | tf_op jit(solution)/shard_map/ppermute | solution.py:260
  251.8 6.9 %collective-permute-start.44 = (f32[4,4,8,128]{3,2,1,0:T(8,128)S(1)}, f32[4,4,8,128]{3,2,1,0:T(8,128)S(1)}, u32[]{:S(2)}, u32[]{:S(2)}) collective-permute-start(f32[4,4,8,128]{3,2,1,0:T(8,128)S(1)} %get-tuple-element.49), channel_id=1, source_target_pairs={{0,8},{8,16},{16,24},{24,0},{1,9},{9,17},{17,25},{25,1},{2,10},{10... | collective-permute-start | bytes 196616 | tf_op jit(solution)/shard_map/ppermute | solution.py:260
  253.8 14.4 %collective-permute-start.46 = (f32[4,4,32,128]{3,2,1,0:T(8,128)S(1)}, f32[4,4,32,128]{3,2,1,0:T(8,128)S(1)}, u32[]{:S(2)}, u32[]{:S(2)}) collective-permute-start(f32[4,4,32,128]{3,2,1,0:T(8,128)S(1)} %get-tuple-element.35), channel_id=1, source_target_pairs={{0,8},{8,16},{16,24},{24,0},{1,9},{9,17},{17,25},{25,1},{2,10},{10... | collective-permute-start | bytes 786440 | tf_op jit(solution)/shard_map/ppermute | solution.py:260
  254.2 13.9 %collective-permute-start.47 = (f32[4,4,32,128]{3,2,1,0:T(8,128)S(1)}, f32[4,4,32,128]{3,2,1,0:T(8,128)S(1)}, u32[]{:S(2)}, u32[]{:S(2)}) collective-permute-start(f32[4,4,32,128]{3,2,1,0:T(8,128)S(1)} %get-tuple-element.36), channel_id=1, source_target_pairs={{0,24},{8,0},{16,8},{24,16},{1,25},{9,1},{17,9},{25,17},{2,26},{10... | collective-permute-start | bytes 786440 | tf_op jit(solution)/shard_map/ppermute | solution.py:260
  257.7 10.5 %collective-permute-start.45 = (f32[4,4,8,128]{3,2,1,0:T(8,128)S(1)}, f32[4,4,8,128]{3,2,1,0:T(8,128)S(1)}, u32[]{:S(2)}, u32[]{:S(2)}) collective-permute-start(f32[4,4,8,128]{3,2,1,0:T(8,128)S(1)} %get-tuple-element.50), channel_id=1, source_target_pairs={{0,24},{8,0},{16,8},{24,16},{1,25},{9,1},{17,9},{25,17},{2,26},{10... | collective-permute-start | bytes 196616 | tf_op jit(solution)/shard_map/ppermute | solution.py:260
  (4 other events, 41.8 us)

commit v2 on v1

--- a/solution.py
+++ b/solution.py
@@ -255,44 +255,148 @@
     return result[0] if one else result
 
 
-def shift(block, axis, step):
-    count = lax.axis_size(axis)
-    return lax.ppermute(block, axis, [(i, (i + step) % count) for i in range(count)])
-
-
-def with_halo(arrays):
-    counts = [a.shape[0] for a in arrays]
-
-    def joined(cut):
-        return jnp.concatenate([cut(a) for a in arrays], 0)
-
-    x_low = shift(joined(lambda a: a[:, -W:]), "gx", 1)
-    x_high = shift(joined(lambda a: a[:, :W]), "gx", -1)
-    y_low = shift(joined(lambda a: a[:, :, -W:]), "gy", 1)
-    y_high = shift(joined(lambda a: a[:, :, :W]), "gy", -1)
-    sides = jnp.concatenate([y_low, y_high], 2)
-    c_low = shift(sides[:, -W:], "gx", 1)
-    c_high = shift(sides[:, :W], "gx", -1)
-    results, at = [], 0
-    for a, n in zip(arrays, counts):
-        s = slice(at, at + n)
-        at += n
-        low = jnp.concatenate([c_low[s, :, :W], y_low[s], c_high[s, :, :W]], 1)
-        high = jnp.concatenate([c_low[s, :, W:], y_high[s], c_high[s, :, W:]], 1)
-        middle = jnp.concatenate([x_low[s], a, x_high[s]], 1)
-        results.append(jnp.concatenate([low, middle, high], 2))
-    return results
-
-
-def gathered(own):
-    whole = lax.all_gather(own[:, :, : L // 2], ("gx", "gy"))
-    nx, ny = lax.axis_size("gx"), lax.axis_size("gy")
-    whole = whole.reshape((nx, ny) + own.shape[:2] + (L // 2,)).transpose(0, 2, 1, 3, 4)
-    whole = whole.reshape(nx * own.shape[0], ny * own.shape[1], L // 2)
-    return jnp.pad(whole, ((0, 0), (0, 0), (0, L // 2)))
-
-
-def local(rhs, coefficient):
+def remote_call(kernel, inputs, outs, scratch, copies, collective_id):
+    return pl.pallas_call(
+        kernel,
+        out_shape=[jax.ShapeDtypeStruct(s, jnp.float32) for s in outs],
+        in_specs=[VMEM] * len(inputs),
+        out_specs=[VMEM] * len(outs),
+        scratch_shapes=[pltpu.VMEM(s, jnp.float32) for s in scratch]
+        + [pltpu.SemaphoreType.DMA((copies,)), pltpu.SemaphoreType.DMA((copies,))],
+        compiler_params=pltpu.CompilerParams(
+            vmem_limit_bytes=48 * 1024 * 1024, collective_id=collective_id, has_side_effects=True
+        ),
+    )(*inputs)
+
+
+def greet(devices):
+    barrier = pltpu.get_barrier_semaphore()
+    for device in devices:
+        pl.semaphore_signal(barrier, inc=1, device_id=device, device_id_type=pl.DeviceIdType.MESH)
+    return barrier, len(devices)
+
+
+SIDES = [(-1, 0), (1, 0), (0, -1), (0, 1), (-1, -1), (-1, 1), (1, -1), (1, 1)]
+
+
+def merged(v):
+    pairs = v.reshape((v.shape[0] // 2, 2) + v.shape[1:])
+    odd = (iota(v.shape[1:], 0) + iota(v.shape[1:], 1)) % 2 == 1
+    return jnp.where(odd, pairs[:, 0], pairs[:, 1])
+
+
+def doubled(m):
+    return jnp.concatenate([m[:, None], m[:, None]], 1).reshape((2 * m.shape[0],) + m.shape[1:])
+
+
+def halo_kernel(dims, merge, n, *refs):
+    ins, outs = refs[:n], refs[n : 2 * n]
+    xs, ys, xr, yr, cr, send_sem, recv_sem = refs[2 * n :]
+    nx, ny = ins[0].shape[1], ins[0].shape[2]
+    me_x, me_y = lax.axis_index("gx"), lax.axis_index("gy")
+    devices = [
+        (lax.rem(me_x + dx + dims[0], dims[0]), lax.rem(me_y + dy + dims[1], dims[1])) for dx, dy in SIDES
+    ]
+    barrier, count = greet(devices)
+    pack = merged if merge else lambda v: v
+    unpack = doubled if merge else lambda v: v
+    at = 0
+    for ref in ins:
+        for c in range(ref.shape[0]):
+            xs[0, at] = pack(ref[c, 0:W])
+            xs[1, at] = pack(ref[c, nx - W : nx])
+            ys[0, at] = pack(ref[c, :, 0:W, :])
+            ys[1, at] = pack(ref[c, :, ny - W : ny, :])
+            at += 1
+    pl.semaphore_wait(barrier, count)
+    w, long = xs.shape[2], ys.shape[2]
+    copies = []
+    for k, (dx, dy) in enumerate(SIDES):
+        sx, sy = int(dx > 0), int(dy > 0)
+        if dy == 0:
+            source, target = xs.at[sx], xr.at[sx]
+        elif dx == 0:
+            source, target = ys.at[sy], yr.at[sy]
+        else:
+            source, target = ys.at[sy, :, pl.ds((long - w) * sx, w)], cr.at[sx, sy]
+        copies.append(
+            pltpu.make_async_remote_copy(
+                src_ref=source, dst_ref=target, send_sem=send_sem.at[k], recv_sem=recv_sem.at[k],
+                device_id=devices[k], device_id_type=pl.DeviceIdType.MESH,
+            )
+        )
+    for copy in copies:
+        copy.start()
+    for ref, out in zip(ins, outs):
+        for c in range(ref.shape[0]):
+            out[c, W : W + nx, W : W + ny, :] = ref[c]
+    for copy in copies:
+        copy.wait()
+    at = 0
+    for out in outs:
+        for c in range(out.shape[0]):
+            for s in range(2):
+                first_x, first_y = (W + nx, W + ny) if s == 0 else (0, 0)
+                out[c, first_x : first_x + W, W : W + ny, :] = unpack(xr[s, at])
+                out[c, W : W + nx, first_y : first_y + W, :] = unpack(yr[s, at])
+                for u in range(2):
+                    corner = W + ny if u == 0 else 0
+                    out[c, first_x : first_x + W, corner : corner + W, :] = unpack(cr[s, u, at])
+            at += 1
+
+
+def with_halo(dims, arrays, collective_id, merge=False):
+    count = sum(a.shape[0] for a in arrays)
+    nx, ny = arrays[0].shape[1], arrays[0].shape[2]
+    w, long = (W // 2, nx // 2) if merge else (W, nx)
+    flat, tall = (2, count, w, ny, L), (2, count, long, W, L)
+    return remote_call(
+        functools.partial(halo_kernel, dims, merge, len(arrays)), arrays,
+        [(a.shape[0], nx + 2 * W, ny + 2 * W, L) for a in arrays],
+        [flat, tall, flat, tall, (2, 2, count, w, W, L)], len(SIDES), collective_id,
+    )
+
+
+def gather_kernel(dims, f_in, c_in, f_out, c_out, slots, send_sem, recv_sem):
+    me_x, me_y = lax.axis_index("gx"), lax.axis_index("gy")
+    along_x = [(lax.rem(me_x + d, dims[0]), me_y) for d in range(1, dims[0])]
+    along_y = [(me_x, lax.rem(me_y + d, dims[1])) for d in range(1, dims[1])]
+    barrier, count = greet(along_x + along_y)
+    half = iota(f_in.shape, 2) < L // 2
+    slots[me_y, me_x] = jnp.where(half, f_in[...], pltpu.roll(c_in[...], L // 2, 2))
+    pl.semaphore_wait(barrier, count)
+    at = 0
+    for devices, part in ((along_x, slots.at[me_y, me_x]), (along_y, slots.at[me_y])):
+        copies = []
+        for device in devices:
+            copies.append(
+                pltpu.make_async_remote_copy(
+                    src_ref=part, dst_ref=part, send_sem=send_sem.at[at], recv_sem=recv_sem.at[at],
+                    device_id=device, device_id_type=pl.DeviceIdType.MESH,
+                )
+            )
+            at += 1
+        for copy in copies:
+            copy.start()
+        for copy in copies:
+            copy.wait()
+    rows, ny = f_out.shape[0], f_in.shape[1]
+    for j in range(dims[1]):
+        part = slots[j].reshape(rows, ny, L)
+        low = iota(part.shape, 2) < L // 2
+        f_out[:, j * ny : (j + 1) * ny, :] = jnp.where(low, part, 0.0)
+        c_out[:, j * ny : (j + 1) * ny, :] = jnp.where(low, pltpu.roll(part, L // 2, 2), 0.0)
+
+
+def gathered(dims, f, coef, collective_id):
+    shape = (f.shape[0] * dims[0], f.shape[1] * dims[1], L)
+    return remote_call(
+        functools.partial(gather_kernel, dims), [f, coef], [shape, shape],
+        [(dims[1], dims[0]) + f.shape], dims[0] + dims[1] - 2, collective_id,
+    )
+
+
+def local(dims, rhs, coefficient):
     shapes = [rhs.shape]
     for _ in range(SPLIT):
         k, a, b, c = shapes[-1]
@@ -306,18 +410,13 @@
         [(s[0], s[1] // 2, s[2], L) for s in shapes[:-1]],
     )
     coefs = [coefficient] + list(coarser)
-    coef_whole = gathered(coefs[SPLIT][0])
 
     source = rhs
     fields, kept = [], []
     for level in range(SPLIT):
         shape = shapes[level]
         ext = extended(shape)
-        if level == 0:
-            f_ext, c_ext = with_halo([source, coefficient])
-        else:
-            (f_ext,) = with_halo([source])
-            (c_ext,) = with_halo([coefs[level]])
+        f_ext, c_ext = with_halo(dims, [source, coefs[level]], level)
         fd, w, v, source = call(
             functools.partial(down_kernel, 0.25**level, L >> level), [f_ext, c_ext],
             [ext, ext, shape, shapes[level + 1]],
@@ -327,7 +426,7 @@
         kept.append((fd, w))
 
     group = L >> SPLIT
-    f_whole = gathered(source[0])
+    f_whole, coef_whole = gathered(dims, source[0], coefs[SPLIT][0], 2 * SPLIT)
     scratch = []
     nx, ny = f_whole.shape[0], f_whole.shape[1]
     for level in range(SPLIT, LEVELS - 1):
@@ -343,7 +442,7 @@
         e, (lax.axis_index("gx") * sx, lax.axis_index("gy") * sy, 0), (sx + 2 * h, sy + 2 * h, L)
     )
     level = SPLIT - 1
-    (t_ext,) = with_halo([fields[level]])
+    (t_ext,) = with_halo(dims, [fields[level]], SPLIT + level, True)
     ext = extended(shapes[level])
     t = call(
         functools.partial(up_last_kernel, 0.25**level, L >> level),
@@ -351,7 +450,7 @@
         [ext, (sx + 2 * h, ext[2], L), (shapes[level][1], 2 * shapes[level][2], L)],
     )
     for level in range(SPLIT - 2, -1, -1):
-        (t_ext,) = with_halo([t])
+        (t_ext,) = with_halo(dims, [t], SPLIT + level, True)
         inputs = [t_ext, *kept[level]]
         ext, shape = extended(shapes[level]), shapes[level]
         if level:
@@ -366,4 +465,5 @@
 
 def solution(mesh):
     spec = P(None, "gx", "gy", None)
-    return jax.shard_map(local, mesh=mesh, in_specs=(spec, spec), out_specs=spec, check_vma=False)
+    dims = (mesh.shape["gx"], mesh.shape["gy"])
+    return jax.shard_map(functools.partial(local, dims), mesh=mesh, in_specs=(spec, spec), out_specs=spec, check_vma=False)

time: 285 us -> 167 us (0.59)
  Pallas kernels: 53.9 us -> 156 us
  blocking collectives: 80 us -> 0 us
  waiting for transfers between devices: 69 us -> 0 us
  starting transfers between devices: 61.3 us -> 0 us
  other arithmetic: 10.4 us -> 0.81 us
    pallas_call x0 -> x7, Pallas kernels: none -> 101 us  [remote_call(): pl.pallas_call(kernel, out_shape=[jax.ShapeDtypeStruct(s, jnp.float32) fo...]
    all_gather x2 -> x0, blocking collectives: 80 us -> none  [gathered(): whole = lax.all_gather(own[:, :, :L // 2], ('gx', 'gy'))]
    ppermute x48 -> x0, waiting for transfers between devices: 69 us -> none  [shift(): lax.ppermute(block, axis, [(i, (i + step) % count) for i in range(count)])]
    ppermute x48 -> x0, starting transfers between devices: 61.3 us -> none  [shift(): lax.ppermute(block, axis, [(i, (i + step) % count) for i in range(count)])]
    concatenate x16 -> x0, other arithmetic: 9.27 us -> none  [the longest x9 5.14 us: with_halo(): results.append(jnp.concatenate([low, middle, high], 2))]
    unnamed x8 -> x24, local copies, waits for them, and re-layouts: 1.77 us -> 9.71 us
    slice x36 -> x0, local copies, waits for them, and re-layouts: 7.54 us -> none  [the longest x8 2.75 us: with_halo(): y_low = shift(joined(lambda a: a[:, :, -W:]), 'gy', 1)]
  transfers between devices with their start and end apart: 48 -> 0, of which waited for: 18 -> 0; matrix products, arithmetic and copies ran while one was open for 5% -> 0% of each run, Pallas kernels for 8% -> 0%
where the time goes in v2:
time: 167 us
  Pallas kernels  156 us (93%)
  local copies, waits for them, and re-layouts  10.3 us (6%)
    pallas_call x7, Pallas kernels, remote_call(): pl.pallas_call(kernel, out_shape=[jax.ShapeDtypeStruct(s, jnp.float32) fo...  101 us
    pallas_call x8, Pallas kernels, call(): pl.pallas_call(kernel, out_shape=shapes, in_specs=[VMEM] * len(inputs), o...  54.3 us
    unnamed x24, local copies, waits for them, and re-layouts  9.71 us

profile of v2, /device:TPU:0, one launch (start us, length us, event | category | flops | bytes accessed | tf_op | source)
XLA Modules:
  0.0 167.0 jit_solution(9418815309293382384)
XLA Ops:
  0.0 0.0 copy-start
  0.0 1.6 copy-done
  1.6 0.0 copy-start.3
  1.6 1.6 copy-done.3
  3.2 39.1 %shard_map.28 = (f32[4,40,40,128]{3,2,1,0:T(8,128)}, f32[4,40,40,128]{3,2,1,0:T(8,128)}) custom-call(f32[4,32,32,128]{3,2,1,0:T(8,128)S(1)} %copy-done.3, f32[4,32,32,128]{3,2,1,0:T(8,128)S(1)} %copy-done), custom_call_target="tpu_custom_call" | custom-call | tf_op jit(solution)/shard_map/pallas_call | solution.py:259
  42.3 0.0 copy-start.1
  42.3 16.8 %shard_map.29 = (f32[4,40,40,128]{3,2,1,0:T(8,128)S(1)}, f32[4,40,40,128]{3,2,1,0:T(8,128)}, f32[4,32,32,128]{3,2,1,0:T(8,128)S(1)}, f32[2,16,16,128]{3,2,1,0:T(8,128)S(1)}) custom-call(f32[4,40,40,128]{3,2,1,0:T(8,128)} %get-tuple-element.28.f_in, f32[4,40,40,128]{3,2,1,0:T(8,128)} %get-tuple-element.29.c_in), custom_call_target="tpu_custom_call" | custom-call | tf_op jit(solution)/shard_map/pallas_call | solution.py:247
  59.1 0.0 copy-start.2
  59.1 1.7 %copy-done.2 = f32[4,40,40,128]{3,2,1,0:T(8,128)} copy-done((f32[4,40,40,128]{3,2,1,0:T(8,128)}, f32[4,40,40,128]{3,2,1,0:T(8,128)S(1)}, u32[]{:S(2)}) %copy-start.2) | copy-done | bytes 3276824
  60.9 0.0 copy-done.1
  60.9 1.2 shard_map.30
  62.0 15.2 %shard_map.31 = (f32[2,24,24,128]{3,2,1,0:T(8,128)S(1)}, f32[2,24,24,128]{3,2,1,0:T(8,128)S(1)}) custom-call(f32[2,16,16,128]{3,2,1,0:T(8,128)S(1)} %get-tuple-element.30.refs_0_, f32[2,16,16,128]{3,2,1,0:T(8,128)S(1)} %get-tuple-element.31.refs_1_), custom_call_target="tpu_custom_call" | custom-call | tf_op jit(solution)/shard_map/pallas_call | solution.py:259
  77.2 5.2 %shard_map.32 = (f32[2,24,24,128]{3,2,1,0:T(8,128)S(1)}, f32[2,24,24,128]{3,2,1,0:T(8,128)S(1)}, f32[2,16,16,128]{3,2,1,0:T(8,128)S(1)}, f32[1,8,8,128]{3,2,1,0:T(8,128)S(1)}) custom-call(f32[2,24,24,128]{3,2,1,0:T(8,128)S(1)} %get-tuple-element.32.f_in, f32[2,24,24,128]{3,2,1,0:T(8,128)S(1)} %get-tuple-element.33.c_in), custom_call_target="tpu_custom_call" | custom-call | tf_op jit(solution)/shard_map/pallas_call | solution.py:247
  82.4 0.0 copy-start.4
  82.4 8.7 %shard_map.33 = (f32[1,16,16,128]{3,2,1,0:T(8,128)S(1)}, f32[1,16,16,128]{3,2,1,0:T(8,128)S(1)}) custom-call(f32[1,8,8,128]{3,2,1,0:T(8,128)S(1)} %get-tuple-element.34.refs_0_, f32[1,8,8,128]{3,2,1,0:T(8,128)S(1)} %get-tuple-element.35.refs_1_), custom_call_target="tpu_custom_call" | custom-call | tf_op jit(solution)/shard_map/pallas_call | solution.py:259
  91.2 2.3 %shard_map.34 = (f32[1,16,16,128]{3,2,1,0:T(8,128)S(1)}, f32[1,16,16,128]{3,2,1,0:T(8,128)S(1)}, f32[1,8,8,128]{3,2,1,0:T(8,128)S(1)}, f32[1,4,4,128]{3,2,1,0:T(4,128)S(1)}) custom-call(f32[1,16,16,128]{3,2,1,0:T(8,128)S(1)} %get-tuple-element.36.f_in, f32[1,16,16,128]{3,2,1,0:T(8,128)S(1)} %get-tuple-element.37.c_in), custom_call_target="tpu_custom_call" | custom-call | tf_op jit(solution)/shard_map/pallas_call | solution.py:247
  93.5 0.0 copy-start.6
  93.5 0.7 copy-done.6
  94.1 0.0 copy-start.10
  94.1 0.6 copy-done.10
  94.8 0.0 copy-start.8
  94.8 8.9 %shard_map.36 = (f32[16,32,128]{2,1,0:T(8,128)S(1)}, f32[16,32,128]{2,1,0:T(8,128)S(1)}) custom-call(f32[4,4,128]{2,1,0:T(4,128)S(1)} %bitcast.3, f32[4,4,128]{2,1,0:T(4,128)S(1)} %bitcast.2), custom_call_target="tpu_custom_call" | custom-call | tf_op jit(solution)/shard_map/pallas_call | solution.py:259
  103.7 0.0 copy-done.4
  103.7 4.7 %shard_map.37 = f32[16,32,128]{2,1,0:T(8,128)S(1)} custom-call(f32[16,32,128]{2,1,0:T(8,128)S(1)} %get-tuple-element.41.f_in, f32[16,32,128]{2,1,0:T(8,128)S(1)} %get-tuple-element.42.c_in), custom_call_target="tpu_custom_call" | custom-call | tf_op jit(solution)/shard_map/pallas_call | solution.py:247
  108.4 0.0 copy-done.8
  108.4 0.6 fusion.8
  109.1 0.8 fusion.3.e_in
  109.9 0.0 copy-start.11
  109.9 0.7 copy-done.11
  110.6 7.3 %shard_map.35.t_in = f32[1,16,16,128]{3,2,1,0:T(8,128)S(1)} custom-call(f32[1,8,8,128]{3,2,1,0:T(8,128)S(1)} %copy-done.11), custom_call_target="tpu_custom_call" | custom-call | tf_op jit(solution)/shard_map/pallas_call | solution.py:259
  118.0 0.0 copy-start.5
  118.0 0.9 copy-done.5
  118.9 0.0 copy-start.7
  118.9 0.9 copy-done.7
  119.8 0.0 copy-start.9
  119.8 0.9 copy-done.9
  120.7 2.8 %shard_map.38.refs_0_ = f32[2,16,16,128]{3,2,1,0:T(8,128)S(1)} custom-call(f32[1,16,16,128]{3,2,1,0:T(8,128)S(1)} %shard_map.35.t_in, f32[8,8,128]{2,1,0:T(8,128)S(1)} %fusion.3.e_in, f32[1,16,16,128]{3,2,1,0:T(8,128)S(1)} %copy-done.7, f32[1,16,16,128]{3,2,1,0:T(8,128)S(1)} %copy-done.9, f32[2,16,16,128]{3,2,1,0:T(8,128)S(1)} %copy-done.5), custom_call_target="tpu_custom_call" | custom-call | tf_op jit(solution)/shard_map/pallas_call | solution.py:247
  123.6 8.8 %shard_map.39.t_in = f32[2,24,24,128]{3,2,1,0:T(8,128)S(1)} custom-call(f32[2,16,16,128]{3,2,1,0:T(8,128)S(1)} %shard_map.38.refs_0_), custom_call_target="tpu_custom_call" | custom-call | tf_op jit(solution)/shard_map/pallas_call | solution.py:259
  132.3 5.5 %shard_map.40.refs_0_ = f32[4,32,32,128]{3,2,1,0:T(8,128)S(1)} custom-call(f32[2,24,24,128]{3,2,1,0:T(8,128)S(1)} %shard_map.39.t_in, f32[2,24,24,128]{3,2,1,0:T(8,128)S(1)} %get-tuple-element.46.f_in, f32[2,24,24,128]{3,2,1,0:T(8,128)S(1)} %get-tuple-element.47.w_in, f32[4,32,32,128]{3,2,1,0:T(8,128)S(1)} %get-tuple-element.48.rest_0_), custom_call_target="tpu_custom_call" | custom-call | tf_op jit(solution)/shard_map/pallas_call | solution.py:247
  137.9 13.4 %shard_map.41.t_in = f32[4,40,40,128]{3,2,1,0:T(8,128)S(1)} custom-call(f32[4,32,32,128]{3,2,1,0:T(8,128)S(1)} %shard_map.40.refs_0_), custom_call_target="tpu_custom_call" | custom-call | tf_op jit(solution)/shard_map/pallas_call | solution.py:259
  151.2 15.8 %shard_map.42 = f32[4,32,32,128]{3,2,1,0:T(8,128)} custom-call(f32[4,40,40,128]{3,2,1,0:T(8,128)S(1)} %shard_map.41.t_in, f32[4,40,40,128]{3,2,1,0:T(8,128)} %copy-done.2, f32[4,40,40,128]{3,2,1,0:T(8,128)} %get-tuple-element.50.w_in), custom_call_target="tpu_custom_call" | custom-call | tf_op jit(solution)/shard_map/pallas_call | solution.py:247
Async XLA Ops:
  0.0 1.6 copy-start
  1.6 1.6 copy-start.3
  42.3 18.5 %copy-start.1 = (f32[4,32,32,128]{3,2,1,0:T(8,128)S(1)}, f32[4,32,32,128]{3,2,1,0:T(8,128)}, u32[]{:S(2)}) copy-start(f32[4,32,32,128]{3,2,1,0:T(8,128)} %c_in.1) | copy-start | bytes 6291460
  59.1 1.7 %copy-start.2 = (f32[4,40,40,128]{3,2,1,0:T(8,128)}, f32[4,40,40,128]{3,2,1,0:T(8,128)S(1)}, u32[]{:S(2)}) copy-start(f32[4,40,40,128]{3,2,1,0:T(8,128)S(1)} %get-tuple-element.49.f_in) | copy-start | bytes 9830404
  82.4 21.3 %copy-start.4 = (f32[2,16,16,128]{3,2,1,0:T(8,128)}, f32[2,16,16,128]{3,2,1,0:T(8,128)S(1)}, u32[]{:S(2)}) copy-start(f32[2,16,16,128]{3,2,1,0:T(8,128)S(1)} %get-tuple-element.45.fine) | copy-start | bytes 786436
  93.5 0.7 copy-start.6
  94.1 0.6 copy-start.10
  94.8 13.7 %copy-start.8 = (f32[1,16,16,128]{3,2,1,0:T(8,128)}, f32[1,16,16,128]{3,2,1,0:T(8,128)S(1)}, u32[]{:S(2)}) copy-start(f32[1,16,16,128]{3,2,1,0:T(8,128)S(1)} %get-tuple-element.44.w_in) | copy-start | bytes 393220
  109.9 0.8 copy-start.11
  118.0 1.0 copy-start.5
  118.9 0.9 copy-start.7
  119.8 0.9 copy-start.9

commit v3 on v2

--- a/solution.py
+++ b/solution.py
@@ -62,33 +62,46 @@
     return outs
 
 
-def half_sweep(v, f_ref, w_ref, colour, low, high, group):
-    count, rows = v.shape[0], v.shape[2]
+def half_sweep(v, f_ref, w_ref, colour, low, high, group, comps=None):
+    rows = v.shape[2]
+    comps = range(v.shape[0]) if comps is None else comps
     parity = (iota((rows, L), 0) + iota((rows, L), 1)) % 2
-
-    def body(step, carry):
-        for k in range(2):
-            x = low + 2 * step + k
+    at_once = 4 if len(comps) == 1 else 2
+
+    def some(start, count):
+        for k in range(count):
+            x = start + k
             mask = parity == (colour + low + k) % 2
-            for c in range(count):
+            for c in comps:
                 mid = v[c, x]
                 total = v[c, x - 1] + v[c, x + 1] + y_sum(mid) + z_sum(mid, group)
                 v[c, x] = jnp.where(mask, f_ref[c, x] + w_ref[c, x] * total, mid)
+
+    def body(step, carry):
+        some(low + at_once * step, at_once)
         return carry
 
-    lax.fori_loop(0, (high - low) // 2, body, 0)
+    steps, left = divmod(high - low, at_once)
+    lax.fori_loop(0, steps, body, 0)
+    if left:
+        some(high - left, left)
 
 
 def down_kernel(scale, group, f_in, c_in, f_out, w_out, v_out, g_out, v, part):
-    count, nx, ny = v_out.shape[0], v_out.shape[1], v_out.shape[2]
-    ex = f_in.shape[1]
-    rows = f_in.shape[2]
+    down(scale, group, range(v.shape[0]), f_in, c_in, f_out, w_out, v_out, v, part)
+    for a, g in enumerate(fold(part, W, v_out.shape[2] // 2)):
+        g_out[a] = g
+
+
+def down(scale, group, comps, f_in, c_in, f_out, w_out, v_out, v, part):
+    nx, ny = v_out.shape[1], v_out.shape[2]
+    ex, rows = f_in.shape[1], f_in.shape[2]
     parity = (iota((rows, L), 0) + iota((rows, L), 1)) % 2
 
     def first(step, carry):
         for k in range(2):
             x = 2 * step + k
-            for c in range(count):
+            for c in comps:
                 inverse = 1.0 / (c_in[c, x] + 6.0 * scale)
                 fd = f_in[c, x] * inverse
                 f_out[c, x] = fd
@@ -97,12 +110,12 @@
         return carry
 
     lax.fori_loop(0, ex // 2, first, 0)
-    half_sweep(v, f_out, w_out, 1, 1, ex - 1, group)
-    half_sweep(v, f_out, w_out, 0, 2, ex - 2, group)
-    half_sweep(v, f_out, w_out, 1, 3, ex - 3, group)
+    half_sweep(v, f_out, w_out, 1, 1, ex - 1, group, comps)
+    half_sweep(v, f_out, w_out, 0, 2, ex - 2, group, comps)
+    half_sweep(v, f_out, w_out, 1, 3, ex - 3, group, comps)
 
     def last(step, carry):
-        for c in range(count):
+        for c in comps:
             total = None
             for k in range(2):
                 x = W + 2 * step + k
@@ -115,53 +128,28 @@
         return carry
 
     lax.fori_loop(0, nx // 2, last, 0)
-    for a, g in enumerate(fold(part, W, ny // 2)):
-        g_out[a] = g
-
-
-def spread(e, half, t):
-    q = dot(e, spread_matrix(half))
-    n = q.shape[0]
-    t[pl.ds(0, n, stride=2), :] = q
-    t[pl.ds(1, n, stride=2), :] = q
-
-
-def post(v, f_ref, w_ref, group):
+
+
+def post(v, f_ref, w_ref, group, comps=None):
     ex = v.shape[1]
     for p, colour in ((1, 0), (2, 1), (3, 0), (4, 1)):
-        half_sweep(v, f_ref, w_ref, colour, p, ex - p, group)
-
-
-def up_kernel(scale, group, t_in, f_in, w_in, *rest):
-    if len(rest) == 2:
-        out, v = rest
-        fine = None
-    else:
-        fine, out, v, t = rest
-    ex = t_in.shape[1]
-
+        half_sweep(v, f_ref, w_ref, colour, p, ex - p, group, comps)
+
+
+def up_kernel(scale, group, t_in, f_in, w_in, fine, out, v, t):
     def copy(x, carry):
         for c in range(t_in.shape[0]):
             v[c, x] = t_in[c, x]
         return carry
 
-    lax.fori_loop(0, ex, copy, 0)
-    finish(v, f_in, w_in, group, fine, out, None if fine is None else t)
+    lax.fori_loop(0, t_in.shape[1], copy, 0)
+    finish(v, f_in, w_in, group, fine, out, t)
 
 
 def finish(v, f_in, w_in, group, fine, out, t):
     post(v, f_in, w_in, group)
     ex, ey = v.shape[1], v.shape[2]
     nx, ny = ex - 2 * W, ey - 2 * W
-    if fine is None:
-
-        def give(x, carry):
-            for c in range(v.shape[0]):
-                out[c, x] = v[c, W + x, W : W + ny, :]
-            return carry
-
-        lax.fori_loop(0, nx, give, 0)
-        return
     for c in range(v.shape[0]):
         for h in range(2):
             q = dot(v[c, W : W + nx, W : W + ny, :].reshape(nx * ny, L), spread_matrix(h)).reshape(nx, ny, L)
@@ -289,71 +277,190 @@
     return jnp.concatenate([m[:, None], m[:, None]], 1).reshape((2 * m.shape[0],) + m.shape[1:])
 
 
-def halo_kernel(dims, merge, n, *refs):
-    ins, outs = refs[:n], refs[n : 2 * n]
-    xs, ys, xr, yr, cr, send_sem, recv_sem = refs[2 * n :]
-    nx, ny = ins[0].shape[1], ins[0].shape[2]
+def ring(dims):
     me_x, me_y = lax.axis_index("gx"), lax.axis_index("gy")
-    devices = [
+    return [
         (lax.rem(me_x + dx + dims[0], dims[0]), lax.rem(me_y + dy + dims[1], dims[1])) for dx, dy in SIDES
     ]
-    barrier, count = greet(devices)
-    pack = merged if merge else lambda v: v
-    unpack = doubled if merge else lambda v: v
-    at = 0
-    for ref in ins:
-        for c in range(ref.shape[0]):
-            xs[0, at] = pack(ref[c, 0:W])
-            xs[1, at] = pack(ref[c, nx - W : nx])
-            ys[0, at] = pack(ref[c, :, 0:W, :])
-            ys[1, at] = pack(ref[c, :, ny - W : ny, :])
-            at += 1
-    pl.semaphore_wait(barrier, count)
-    w, long = xs.shape[2], ys.shape[2]
-    copies = []
-    for k, (dx, dy) in enumerate(SIDES):
-        sx, sy = int(dx > 0), int(dy > 0)
-        if dy == 0:
-            source, target = xs.at[sx], xr.at[sx]
-        elif dx == 0:
-            source, target = ys.at[sy], yr.at[sy]
-        else:
-            source, target = ys.at[sy, :, pl.ds((long - w) * sx, w)], cr.at[sx, sy]
-        copies.append(
-            pltpu.make_async_remote_copy(
-                src_ref=source, dst_ref=target, send_sem=send_sem.at[k], recv_sem=recv_sem.at[k],
-                device_id=devices[k], device_id_type=pl.DeviceIdType.MESH,
+
+
+BUFFERS = 7
+
+
+def halo_scratch(count, nx, ny, merge):
+    w, long = (W // 2, nx // 2) if merge else (W, nx)
+    flat, tall = (2, count, w, ny, L), (2, count, long, W, L)
+    shapes = [flat, tall, flat, tall, (2, 2, count, w, W, L)]
+    return [pltpu.VMEM(s, jnp.float32) for s in shapes] + [pltpu.SemaphoreType.DMA((len(SIDES),))] * 2
+
+
+class Halo:
+    def __init__(self, devices, merge, sources, targets, buffers):
+        self.merge, self.sources, self.targets = merge, sources, targets
+        self.xs, self.ys, self.xr, self.yr, self.cr, send_sem, recv_sem = buffers
+        self.nx, self.ny = sources[0][0].shape[1], sources[0][0].shape[2]
+        w, long = self.xs.shape[2], self.ys.shape[2]
+        self.copies = []
+        for k, (dx, dy) in enumerate(SIDES):
+            sx, sy = int(dx > 0), int(dy > 0)
+            if dy == 0:
+                source, target = self.xs.at[sx], self.xr.at[sx]
+            elif dx == 0:
+                source, target = self.ys.at[sy], self.yr.at[sy]
+            else:
+                source, target = self.ys.at[sy, :, pl.ds((long - w) * sx, w)], self.cr.at[sx, sy]
+            self.copies.append(
+                pltpu.make_async_remote_copy(
+                    src_ref=source, dst_ref=target, send_sem=send_sem.at[k], recv_sem=recv_sem.at[k],
+                    device_id=devices[k], device_id_type=pl.DeviceIdType.MESH,
+                )
             )
-        )
-    for copy in copies:
-        copy.start()
-    for ref, out in zip(ins, outs):
-        for c in range(ref.shape[0]):
-            out[c, W : W + nx, W : W + ny, :] = ref[c]
-    for copy in copies:
-        copy.wait()
-    at = 0
-    for out in outs:
-        for c in range(out.shape[0]):
+
+    def stage(self):
+        pack = merged if self.merge else lambda v: v
+        nx, ny = self.nx, self.ny
+        for at, (ref, c) in enumerate(self.sources):
+            self.xs[0, at] = pack(ref[c, 0:W])
+            self.xs[1, at] = pack(ref[c, nx - W : nx])
+            self.ys[0, at] = pack(ref[c, :, 0:W, :])
+            self.ys[1, at] = pack(ref[c, :, ny - W : ny, :])
+
+    def start(self):
+        for copy in self.copies:
+            copy.start()
+
+    def middle(self):
+        for (ref, c), (out, d) in zip(self.sources, self.targets):
+            out[d, W : W + self.nx, W : W + self.ny, :] = ref[c]
+
+    def wait(self):
+        for copy in self.copies:
+            copy.wait()
+
+    def edges(self):
+        unpack = doubled if self.merge else lambda v: v
+        nx, ny = self.nx, self.ny
+        for at, (out, c) in enumerate(self.targets):
             for s in range(2):
                 first_x, first_y = (W + nx, W + ny) if s == 0 else (0, 0)
-                out[c, first_x : first_x + W, W : W + ny, :] = unpack(xr[s, at])
-                out[c, W : W + nx, first_y : first_y + W, :] = unpack(yr[s, at])
+                out[c, first_x : first_x + W, W : W + ny, :] = unpack(self.xr[s, at])
+                out[c, W : W + nx, first_y : first_y + W, :] = unpack(self.yr[s, at])
                 for u in range(2):
                     corner = W + ny if u == 0 else 0
-                    out[c, first_x : first_x + W, corner : corner + W, :] = unpack(cr[s, u, at])
-            at += 1
+                    out[c, first_x : first_x + W, corner : corner + W, :] = unpack(self.cr[s, u, at])
+
+
+def pairs_of(refs):
+    return [(ref, c) for ref in refs for c in range(ref.shape[0])]
+
+
+def halo_kernel(dims, merge, n, *refs):
+    devices = ring(dims)
+    barrier, count = greet(devices)
+    halo = Halo(devices, merge, pairs_of(refs[:n]), pairs_of(refs[n : 2 * n]), refs[2 * n :])
+    halo.stage()
+    pl.semaphore_wait(barrier, count)
+    halo.start()
+    halo.middle()
+    halo.wait()
+    halo.edges()
+
+
+def in_turn(halos, work, tail):
+    halos[0].start()
+    for k, halo in enumerate(halos):
+        if k + 1 < len(halos):
+            halos[k + 1].stage()
+        halo.middle()
+        halo.wait()
+        if k + 1 < len(halos):
+            halos[k + 1].start()
+        else:
+            for other in tail:
+                other.start()
+        halo.edges()
+        work(k)
+    for other in tail:
+        other.middle()
+        other.wait()
+        other.edges()
+
+
+def first_down_kernel(dims, splits, *refs):
+    f_in, c_in = refs[:2]
+    coarse = refs[2 : 2 + splits]
+    f_out, w_out, v_out, g_out = refs[2 + splits : 6 + splits]
+    coarse_out = refs[6 + splits : 6 + 2 * splits]
+    f_ext, c_ext, v, part = refs[6 + 2 * splits : 10 + 2 * splits]
+    rest = refs[10 + 2 * splits :]
+    devices = ring(dims)
+    barrier, count = greet(devices)
+    parts = f_in.shape[0]
+    halos = [
+        Halo(
+            devices, False, [(f_in, c), (c_in, c)], [(f_ext, c), (c_ext, c)],
+            rest[BUFFERS * c : BUFFERS * (c + 1)],
+        )
+        for c in range(parts)
+    ]
+    tail = [
+        Halo(
+            devices, False, pairs_of([coarse[i]]), pairs_of([coarse_out[i]]),
+            rest[BUFFERS * (parts + i) : BUFFERS * (parts + i + 1)],
+        )
+        for i in range(splits)
+    ]
+    halos[0].stage()
+    pl.semaphore_wait(barrier, count)
+    for other in tail:
+        other.stage()
+
+    def work(c):
+        down(1.0, L, [c], f_ext, c_ext, f_out, w_out, v_out, v, part)
+
+    in_turn(halos, work, tail)
+    for a, g in enumerate(fold(part, W, v_out.shape[2] // 2)):
+        g_out[a] = g
+
+
+def last_up_kernel(dims, t_in, f_in, w_in, out, v, *rest):
+    devices = ring(dims)
+    barrier, count = greet(devices)
+    parts, nx, ny = out.shape[0], out.shape[1], out.shape[2]
+    halos = [
+        Halo(devices, True, [(t_in, c)], [(v, c)], rest[BUFFERS * c : BUFFERS * (c + 1)])
+        for c in range(parts)
+    ]
+    halos[0].stage()
+    pl.semaphore_wait(barrier, count)
+
+    def work(c):
+        post(v, f_in, w_in, L, [c])
+        out[c] = v[c, W : W + nx, W : W + ny, :]
+
+    in_turn(halos, work, [])
+
+
+def remote_kernel(kernel, inputs, outs, scratch, collective_id):
+    return pl.pallas_call(
+        kernel,
+        out_shape=[jax.ShapeDtypeStruct(s, jnp.float32) for s in outs],
+        in_specs=[VMEM] * len(inputs),
+        out_specs=[VMEM] * len(outs),
+        scratch_shapes=scratch,
+        compiler_params=pltpu.CompilerParams(
+            vmem_limit_bytes=48 * 1024 * 1024, collective_id=collective_id, has_side_effects=True
+        ),
+    )(*inputs)
 
 
 def with_halo(dims, arrays, collective_id, merge=False):
     count = sum(a.shape[0] for a in arrays)
     nx, ny = arrays[0].shape[1], arrays[0].shape[2]
-    w, long = (W // 2, nx // 2) if merge else (W, nx)
-    flat, tall = (2, count, w, ny, L), (2, count, long, W, L)
-    return remote_call(
+    return remote_kernel(
         functools.partial(halo_kernel, dims, merge, len(arrays)), arrays,
         [(a.shape[0], nx + 2 * W, ny + 2 * W, L) for a in arrays],
-        [flat, tall, flat, tall, (2, 2, count, w, W, L)], len(SIDES), collective_id,
+        halo_scratch(count, nx, ny, merge), collective_id,
     )
 
 
@@ -416,12 +523,23 @@
     for level in range(SPLIT):
         shape = shapes[level]
         ext = extended(shape)
-        f_ext, c_ext = with_halo(dims, [source, coefs[level]], level)
-        fd, w, v, source = call(
-            functools.partial(down_kernel, 0.25**level, L >> level), [f_ext, c_ext],
-            [ext, ext, shape, shapes[level + 1]],
-            [ext, (shape[0], shape[1] // 2, ext[2], L)],
-        )
+        wide_part = (shape[0], shape[1] // 2, ext[2], L)
+        if level == 0:
+            scratch = [pltpu.VMEM(x, jnp.float32) for x in (ext, ext, ext, wide_part)]
+            for _ in range(shape[0]):
+                scratch += halo_scratch(2, shape[1], shape[2], False)
+            for x in shapes[1:SPLIT]:
+                scratch += halo_scratch(x[0], x[1], x[2], False)
+            fd, w, v, source, *c_exts = remote_kernel(
+                functools.partial(first_down_kernel, dims, SPLIT - 1), [source] + coefs[:SPLIT],
+                [ext, ext, shape, shapes[1]] + [extended(x) for x in shapes[1:SPLIT]], scratch, 0,
+            )
+        else:
+            (f_ext,) = with_halo(dims, [source], level)
+            fd, w, v, source = call(
+                functools.partial(down_kernel, 0.25**level, L >> level), [f_ext, c_exts[level - 1]],
+                [ext, ext, shape, shapes[level + 1]], [ext, wide_part],
+            )
         fields.append(v)
         kept.append((fd, w))
 
@@ -449,18 +567,20 @@
         [t_ext, e, *kept[level], fields[level - 1]], shapes[level - 1],
         [ext, (sx + 2 * h, ext[2], L), (shapes[level][1], 2 * shapes[level][2], L)],
     )
-    for level in range(SPLIT - 2, -1, -1):
+    for level in range(SPLIT - 2, 0, -1):
         (t_ext,) = with_halo(dims, [t], SPLIT + level, True)
-        inputs = [t_ext, *kept[level]]
         ext, shape = extended(shapes[level]), shapes[level]
-        if level:
-            t = call(
-                functools.partial(up_kernel, 0.25**level, L >> level), inputs + [fields[level - 1]],
-                shapes[level - 1], [ext, (shape[1], 2 * shape[2], L)],
-            )
-        else:
-            t = call(functools.partial(up_kernel, 1.0, L), inputs, shape, [ext])
-    return t
+        t = call(
+            functools.partial(up_kernel, 0.25**level, L >> level), [t_ext, *kept[level], fields[level - 1]],
+            shapes[level - 1], [ext, (shape[1], 2 * shape[2], L)],
+        )
+    shape = shapes[0]
+    scratch = [pltpu.VMEM(extended(shape), jnp.float32)]
+    for _ in range(shape[0]):
+        scratch += halo_scratch(1, shape[1], shape[2], True)
+    return remote_kernel(
+        functools.partial(last_up_kernel, dims), [t, *kept[0]], [shape], scratch, SPLIT
+    )[0]
 
 
 def solution(mesh):

time: 167 us -> 157 us (0.940)
  local copies, waits for them, and re-layouts: 10.3 us -> 3.36 us
  Pallas kernels: 156 us -> 153 us
    pallas_call x0 -> x6, Pallas kernels: none -> 123 us  [remote_kernel(): pl.pallas_call(kernel, out_shape=[jax.ShapeDtypeStruct(s, jnp.float32) fo...]
    pallas_call x7 -> x1, Pallas kernels: 101 us -> 9.66 us  [remote_call(): pl.pallas_call(kernel, out_shape=[jax.ShapeDtypeStruct(s, jnp.float32) fo...]
    pallas_call x8 -> x6, Pallas kernels: 54.3 us -> 20.3 us  [call(): pl.pallas_call(kernel, out_shape=shapes, in_specs=[VMEM] * len(inputs), o...]
    unnamed x24 -> x5, local copies, waits for them, and re-layouts: 9.71 us -> 3.35 us
where the time goes in v3:
time: 157 us; the launch traced here: 156 us
  Pallas kernels  153 us (97%)
  local copies, waits for them, and re-layouts  3.36 us (2%)
    pallas_call x6, Pallas kernels, remote_kernel(): pl.pallas_call(kernel, out_shape=[jax.ShapeDtypeStruct(s, jnp.float32) fo...  123 us
    pallas_call x6, Pallas kernels, call(): pl.pallas_call(kernel, out_shape=shapes, in_specs=[VMEM] * len(inputs), o...  20.3 us
    pallas_call x1, Pallas kernels, remote_call(): pl.pallas_call(kernel, out_shape=[jax.ShapeDtypeStruct(s, jnp.float32) fo...  9.66 us
    unnamed x5, local copies, waits for them, and re-layouts  3.35 us

profile of v3, /device:TPU:0, one launch (start us, length us, event | category | flops | bytes accessed | tf_op | source)
XLA Modules:
  0.0 156.4 jit_solution(13579711273325608826)
XLA Ops:
  0.0 0.0 copy-start
  0.0 1.6 %copy-done = f32[4,32,32,128]{3,2,1,0:T(8,128)S(1)} copy-done((f32[4,32,32,128]{3,2,1,0:T(8,128)S(1)}, f32[4,32,32,128]{3,2,1,0:T(8,128)}, u32[]{:S(2)}) %copy-start) | copy-done | bytes 2097176
  1.6 0.0 copy-start.1
  1.6 1.2 shard_map.28
  2.7 0.4 copy-done.1
  3.2 58.4 %shard_map.29 = (f32[4,40,40,128]{3,2,1,0:T(8,128)}, f32[4,40,40,128]{3,2,1,0:T(8,128)}, f32[4,32,32,128]{3,2,1,0:T(8,128)S(1)}, f32[2,16,16,128]{3,2,1,0:T(8,12...) custom-call(f32[4,32,32,128]{3,2,1,0:T(8,128)S(1)} %copy-done.1, f32[4,32,32,128]{3,2,1,0:T(8,128)} %refs_1_.1, ...), custom_call_target="tpu_custom_call" | custom-call | tf_op jit(solution)/shard_map/pallas_call | solution.py:445
  61.6 10.6 %shard_map.30.f_in = f32[2,24,24,128]{3,2,1,0:T(8,128)S(1)} custom-call(f32[2,16,16,128]{3,2,1,0:T(8,128)S(1)} %get-tuple-element.26.refs_0_), custom_call_target="tpu_custom_call" | custom-call | tf_op jit(solution)/shard_map/pallas_call | solution.py:445
  72.2 5.2 %shard_map.31 = (f32[2,24,24,128]{3,2,1,0:T(8,128)S(1)}, f32[2,24,24,128]{3,2,1,0:T(8,128)S(1)}, f32[2,16,16,128]{3,2,1,0:T(8,128)S(1)}, f32[1,8,8,128]{3,2,1,0:T(8,128)S(1)}) custom-call(f32[2,24,24,128]{3,2,1,0:T(8,128)S(1)} %shard_map.30.f_in, f32[2,24,24,128]{3,2,1,0:T(8,128)S(1)} %get-tuple-element.27.c_in), custom_call_target="tpu_custom_call" | custom-call | tf_op jit(solution)/shard_map/pallas_call | solution.py:235
  77.4 7.5 %shard_map.32.f_in = f32[1,16,16,128]{3,2,1,0:T(8,128)S(1)} custom-call(f32[1,8,8,128]{3,2,1,0:T(8,128)S(1)} %get-tuple-element.28.refs_0_), custom_call_target="tpu_custom_call" | custom-call | tf_op jit(solution)/shard_map/pallas_call | solution.py:445
  84.9 1.7 %shard_map.33 = (f32[1,16,16,128]{3,2,1,0:T(8,128)S(1)}, f32[1,16,16,128]{3,2,1,0:T(8,128)S(1)}, f32[1,8,8,128]{3,2,1,0:T(8,128)S(1)}, f32[1,4,4,128]{3,2,1,0:T(4,128)S(1)}) custom-call(f32[1,16,16,128]{3,2,1,0:T(8,128)S(1)} %shard_map.32.f_in, f32[1,16,16,128]{3,2,1,0:T(8,128)S(1)} %get-tuple-element.29.c_in), custom_call_target="tpu_custom_call" | custom-call | tf_op jit(solution)/shard_map/pallas_call | solution.py:235
  86.6 7.1 %shard_map.34.t_in = f32[1,16,16,128]{3,2,1,0:T(8,128)S(1)} custom-call(f32[1,8,8,128]{3,2,1,0:T(8,128)S(1)} %get-tuple-element.30.refs_0_), custom_call_target="tpu_custom_call" | custom-call | tf_op jit(solution)/shard_map/pallas_call | solution.py:445
  93.7 9.7 %shard_map.35 = (f32[16,32,128]{2,1,0:T(8,128)S(1)}, f32[16,32,128]{2,1,0:T(8,128)S(1)}) custom-call(f32[4,4,128]{2,1,0:T(4,128)S(1)} %bitcast.3, f32[4,4,128]{2,1,0:T(4,128)S(1)} %bitcast.2), custom_call_target="tpu_custom_call" | custom-call | tf_op jit(solution)/shard_map/pallas_call | solution.py:247
  103.4 4.7 %shard_map.36 = f32[16,32,128]{2,1,0:T(8,128)S(1)} custom-call(f32[16,32,128]{2,1,0:T(8,128)S(1)} %get-tuple-element.33.f_in, f32[16,32,128]{2,1,0:T(8,128)S(1)} %get-tuple-element.34.c_in), custom_call_target="tpu_custom_call" | custom-call | tf_op jit(solution)/shard_map/pallas_call | solution.py:235
  108.1 0.1 fusion.3.e_in
  108.2 2.0 %shard_map.37.refs_0_ = f32[2,16,16,128]{3,2,1,0:T(8,128)S(1)} custom-call(f32[1,16,16,128]{3,2,1,0:T(8,128)S(1)} %shard_map.34.t_in, f32[8,8,128]{2,1,0:T(8,128)S(1)} %fusion.3.e_in, f32[1,16,16,128]{3,2,1,0:T(8,128)S(1)} %get-tuple-element.35.f_in, f32[1,16,16,128]{3,2,1,0:T(8,128)S(1)} %get-tuple-element.36.w_in, ...), custom_call_target="tpu_custom_call" | custom-call | tf_op jit(solution)/shard_map/pallas_call | solution.py:235
  110.3 8.8 %shard_map.38.t_in = f32[2,24,24,128]{3,2,1,0:T(8,128)S(1)} custom-call(f32[2,16,16,128]{3,2,1,0:T(8,128)S(1)} %shard_map.37.refs_0_), custom_call_target="tpu_custom_call" | custom-call | tf_op jit(solution)/shard_map/pallas_call | solution.py:445
  119.1 5.5 %shard_map.39.t_in = f32[4,32,32,128]{3,2,1,0:T(8,128)S(1)} custom-call(f32[2,24,24,128]{3,2,1,0:T(8,128)S(1)} %shard_map.38.t_in, f32[2,24,24,128]{3,2,1,0:T(8,128)S(1)} %get-tuple-element.38.f_in, f32[2,24,24,128]{3,2,1,0:T(8,128)S(1)} %get-tuple-element.39.w_in, f32[4,32,32,128]{3,2,1,0:T(8,128)S(1)} %get-tuple-element.40.fine), custom_call_target="tpu_custom_call" | custom-call | tf_op jit(solution)/shard_map/pallas_call | solution.py:235
  124.7 30.4 %shard_map.40 = f32[4,32,32,128]{3,2,1,0:T(8,128)S(1)} custom-call(f32[4,32,32,128]{3,2,1,0:T(8,128)S(1)} %shard_map.39.t_in, f32[4,40,40,128]{3,2,1,0:T(8,128)} %get-tuple-element.41.f_in, f32[4,40,40,128]{3,2,1,0:T(8,128)} %get-tuple-element.42.w_in), custom_call_target="tpu_custom_call" | custom-call | tf_op jit(solution)/shard_map/pallas_call | solution.py:445
  155.0 1.3 copy.4
  (1 shorter events, 0.0 us)
Async XLA Ops:
  0.0 1.6 %copy-start = (f32[4,32,32,128]{3,2,1,0:T(8,128)S(1)}, f32[4,32,32,128]{3,2,1,0:T(8,128)}, u32[]{:S(2)}) copy-start(f32[4,32,32,128]{3,2,1,0:T(8,128)} %refs_1_.1) | copy-start | bytes 6291460
  1.6 1.6 %copy-start.1 = (f32[4,32,32,128]{3,2,1,0:T(8,128)S(1)}, f32[4,32,32,128]{3,2,1,0:T(8,128)}, u32[]{:S(2)}) copy-start(f32[4,32,32,128]{3,2,1,0:T(8,128)} %refs_0_.1) | copy-start | bytes 6291460

commit v4 on v3

--- a/solution.py
+++ b/solution.py
@@ -241,20 +241,6 @@
         compiler_params=pltpu.CompilerParams(vmem_limit_bytes=48 * 1024 * 1024),
     )(*inputs)
     return result[0] if one else result
-
-
-def remote_call(kernel, inputs, outs, scratch, copies, collective_id):
-    return pl.pallas_call(
-        kernel,
-        out_shape=[jax.ShapeDtypeStruct(s, jnp.float32) for s in outs],
-        in_specs=[VMEM] * len(inputs),
-        out_specs=[VMEM] * len(outs),
-        scratch_shapes=[pltpu.VMEM(s, jnp.float32) for s in scratch]
-        + [pltpu.SemaphoreType.DMA((copies,)), pltpu.SemaphoreType.DMA((copies,))],
-        compiler_params=pltpu.CompilerParams(
-            vmem_limit_bytes=48 * 1024 * 1024, collective_id=collective_id, has_side_effects=True
-        ),
-    )(*inputs)
 
 
 def greet(devices):
@@ -366,16 +352,19 @@
     halo.edges()
 
 
-def in_turn(halos, work, tail):
-    halos[0].start()
+def in_turn(halos, ahead, work, tail):
+    for k in range(ahead):
+        if k:
+            halos[k].stage()
+        halos[k].start()
     for k, halo in enumerate(halos):
-        if k + 1 < len(halos):
-            halos[k + 1].stage()
+        if k + ahead < len(halos):
+            halos[k + ahead].stage()
         halo.middle()
         halo.wait()
-        if k + 1 < len(halos):
-            halos[k + 1].start()
-        else:
+        if k + ahead < len(halos):
+            halos[k + ahead].start()
+        if k + 1 == len(halos):
             for other in tail:
                 other.start()
         halo.edges()
@@ -418,7 +407,7 @@
     def work(c):
         down(1.0, L, [c], f_ext, c_ext, f_out, w_out, v_out, v, part)
 
-    in_turn(halos, work, tail)
+    in_turn(halos, min(2, parts), work, tail)
     for a, g in enumerate(fold(part, W, v_out.shape[2] // 2)):
         g_out[a] = g
 
@@ -438,7 +427,7 @@
         post(v, f_in, w_in, L, [c])
         out[c] = v[c, W : W + nx, W : W + ny, :]
 
-    in_turn(halos, work, [])
+    in_turn(halos, parts, work, [])
 
 
 def remote_kernel(kernel, inputs, outs, scratch, collective_id):
@@ -464,18 +453,21 @@
     )
 
 
-def gather_kernel(dims, f_in, c_in, f_out, c_out, slots, send_sem, recv_sem):
+def gather_kernel(dims, f_in, c_in, t_in, f_out, c_out, t_out, slots, send_sem, recv_sem, *buffers):
     me_x, me_y = lax.axis_index("gx"), lax.axis_index("gy")
     along_x = [(lax.rem(me_x + d, dims[0]), me_y) for d in range(1, dims[0])]
     along_y = [(me_x, lax.rem(me_y + d, dims[1])) for d in range(1, dims[1])]
-    barrier, count = greet(along_x + along_y)
+    devices = ring(dims)
+    barrier, count = greet(along_x + along_y + devices[4:])
+    halo = Halo(devices, True, pairs_of([t_in]), pairs_of([t_out]), buffers)
+    halo.stage()
     half = iota(f_in.shape, 2) < L // 2
     slots[me_y, me_x] = jnp.where(half, f_in[...], pltpu.roll(c_in[...], L // 2, 2))
     pl.semaphore_wait(barrier, count)
     at = 0
-    for devices, part in ((along_x, slots.at[me_y, me_x]), (along_y, slots.at[me_y])):
+    for others, part in ((along_x, slots.at[me_y, me_x]), (along_y, slots.at[me_y])):
         copies = []
-        for device in devices:
+        for device in others:
             copies.append(
                 pltpu.make_async_remote_copy(
                     src_ref=part, dst_ref=part, send_sem=send_sem.at[at], recv_sem=recv_sem.at[at],
@@ -485,21 +477,32 @@
             at += 1
         for copy in copies:
             copy.start()
+        if others is along_x:
+            halo.middle()
         for copy in copies:
             copy.wait()
+        if others is along_x:
+            halo.start()
     rows, ny = f_out.shape[0], f_in.shape[1]
     for j in range(dims[1]):
         part = slots[j].reshape(rows, ny, L)
         low = iota(part.shape, 2) < L // 2
         f_out[:, j * ny : (j + 1) * ny, :] = jnp.where(low, part, 0.0)
         c_out[:, j * ny : (j + 1) * ny, :] = jnp.where(low, pltpu.roll(part, L // 2, 2), 0.0)
-
-
-def gathered(dims, f, coef, collective_id):
+    halo.wait()
+    halo.edges()
+
+
+def gathered(dims, f, coef, t, collective_id):
     shape = (f.shape[0] * dims[0], f.shape[1] * dims[1], L)
-    return remote_call(
-        functools.partial(gather_kernel, dims), [f, coef], [shape, shape],
-        [(dims[1], dims[0]) + f.shape], dims[0] + dims[1] - 2, collective_id,
+    copies = dims[0] + dims[1] - 2
+    return remote_kernel(
+        functools.partial(gather_kernel, dims), [f, coef, t],
+        [shape, shape, (t.shape[0], t.shape[1] + 2 * W, t.shape[2] + 2 * W, L)],
+        [pltpu.VMEM((dims[1], dims[0]) + f.shape, jnp.float32)]
+        + [pltpu.SemaphoreType.DMA((copies,))] * 2
+        + halo_scratch(t.shape[0], t.shape[1], t.shape[2], True),
+        collective_id,
     )
 
 
@@ -544,7 +547,7 @@
         kept.append((fd, w))
 
     group = L >> SPLIT
-    f_whole, coef_whole = gathered(dims, source[0], coefs[SPLIT][0], 2 * SPLIT)
+    f_whole, coef_whole, t_ext = gathered(dims, source[0], coefs[SPLIT][0], fields[-1], 2 * SPLIT)
     scratch = []
     nx, ny = f_whole.shape[0], f_whole.shape[1]
     for level in range(SPLIT, LEVELS - 1):
@@ -560,7 +563,6 @@
         e, (lax.axis_index("gx") * sx, lax.axis_index("gy") * sy, 0), (sx + 2 * h, sy + 2 * h, L)
     )
     level = SPLIT - 1
-    (t_ext,) = with_halo(dims, [fields[level]], SPLIT + level, True)
     ext = extended(shapes[level])
     t = call(
         functools.partial(up_last_kernel, 0.25**level, L >> level),

time: 157 us -> 141 us (0.90)
  Pallas kernels: 153 us -> 137 us
    pallas_call x1 -> x0, Pallas kernels: 9.66 us -> none  [remote_call(): pl.pallas_call(kernel, out_shape=[jax.ShapeDtypeStruct(s, jnp.float32) fo...]
    pallas_call x6, Pallas kernels: 123 us -> 117 us  [remote_kernel(): pl.pallas_call(kernel, out_shape=[jax.ShapeDtypeStruct(s, jnp.float32) fo...]
where the time goes in v4:
time: 141 us
  Pallas kernels  137 us (97%)
  local copies, waits for them, and re-layouts  3.36 us (2%)
    pallas_call x6, Pallas kernels, remote_kernel(): pl.pallas_call(kernel, out_shape=[jax.ShapeDtypeStruct(s, jnp.float32) fo...  117 us
    pallas_call x6, Pallas kernels, call(): pl.pallas_call(kernel, out_shape=shapes, in_specs=[VMEM] * len(inputs), o...  20.3 us
    unnamed x5, local copies, waits for them, and re-layouts  3.35 us

profile of v4, /device:TPU:0, one launch (start us, length us, event | category | flops | bytes accessed | tf_op | source)
XLA Modules:
  0.0 140.8 jit_solution(16666973287066907970)
XLA Ops:
  0.0 0.0 copy-start
  0.0 1.6 %copy-done = f32[4,32,32,128]{3,2,1,0:T(8,128)S(1)} copy-done((f32[4,32,32,128]{3,2,1,0:T(8,128)S(1)}, f32[4,32,32,128]{3,2,1,0:T(8,128)}, u32[]{:S(2)}) %copy-start) | copy-done | bytes 2097176
  1.6 0.0 copy-start.1
  1.6 1.2 shard_map.28
  2.7 0.4 copy-done.1
  3.2 50.9 %shard_map.29 = (f32[4,40,40,128]{3,2,1,0:T(8,128)}, f32[4,40,40,128]{3,2,1,0:T(8,128)}, f32[4,32,32,128]{3,2,1,0:T(8,128)S(1)}, f32[2,16,16,128]{3,2,1,0:T(8,12...) custom-call(f32[4,32,32,128]{3,2,1,0:T(8,128)S(1)} %copy-done.1, f32[4,32,32,128]{3,2,1,0:T(8,128)} %refs_1_.1, ...), custom_call_target="tpu_custom_call" | custom-call | tf_op jit(solution)/shard_map/pallas_call | solution.py:434
  54.1 10.9 %shard_map.30.f_in = f32[2,24,24,128]{3,2,1,0:T(8,128)S(1)} custom-call(f32[2,16,16,128]{3,2,1,0:T(8,128)S(1)} %get-tuple-element.27.refs_0_), custom_call_target="tpu_custom_call" | custom-call | tf_op jit(solution)/shard_map/pallas_call | solution.py:434
  64.9 5.2 %shard_map.31 = (f32[2,24,24,128]{3,2,1,0:T(8,128)S(1)}, f32[2,24,24,128]{3,2,1,0:T(8,128)S(1)}, f32[2,16,16,128]{3,2,1,0:T(8,128)S(1)}, f32[1,8,8,128]{3,2,1,0:T(8,128)S(1)}) custom-call(f32[2,24,24,128]{3,2,1,0:T(8,128)S(1)} %shard_map.30.f_in, f32[2,24,24,128]{3,2,1,0:T(8,128)S(1)} %get-tuple-element.28.c_in), custom_call_target="tpu_custom_call" | custom-call | tf_op jit(solution)/shard_map/pallas_call | solution.py:235
  70.1 7.6 %shard_map.32.f_in = f32[1,16,16,128]{3,2,1,0:T(8,128)S(1)} custom-call(f32[1,8,8,128]{3,2,1,0:T(8,128)S(1)} %get-tuple-element.29.refs_0_), custom_call_target="tpu_custom_call" | custom-call | tf_op jit(solution)/shard_map/pallas_call | solution.py:434
  77.7 1.7 %shard_map.33 = (f32[1,16,16,128]{3,2,1,0:T(8,128)S(1)}, f32[1,16,16,128]{3,2,1,0:T(8,128)S(1)}, f32[1,8,8,128]{3,2,1,0:T(8,128)S(1)}, f32[1,4,4,128]{3,2,1,0:T(4,128)S(1)}) custom-call(f32[1,16,16,128]{3,2,1,0:T(8,128)S(1)} %shard_map.32.f_in, f32[1,16,16,128]{3,2,1,0:T(8,128)S(1)} %get-tuple-element.30.c_in), custom_call_target="tpu_custom_call" | custom-call | tf_op jit(solution)/shard_map/pallas_call | solution.py:235
  79.4 10.3 %shard_map.34 = (f32[16,32,128]{2,1,0:T(8,128)S(1)}, f32[16,32,128]{2,1,0:T(8,128)S(1)}, f32[1,16,16,128]{3,2,1,0:T(8,128)S(1)}) custom-call(f32[4,4,128]{2,1,0:T(4,128)S(1)} %bitcast.3, f32[4,4,128]{2,1,0:T(4,128)S(1)} %bitcast.2, f32[1,8,8,128]{3,2,1,0:T(8,128)S(1)} %get-tuple-element.33.t_in), custom_call_target="tpu_custom_call" | custom-call | tf_op jit(solution)/shard_map/pallas_call | solution.py:434
  89.7 4.7 %shard_map.35 = f32[16,32,128]{2,1,0:T(8,128)S(1)} custom-call(f32[16,32,128]{2,1,0:T(8,128)S(1)} %get-tuple-element.35.f_in, f32[16,32,128]{2,1,0:T(8,128)S(1)} %get-tuple-element.36.c_in), custom_call_target="tpu_custom_call" | custom-call | tf_op jit(solution)/shard_map/pallas_call | solution.py:235
  94.4 0.1 fusion.3.e_in
  94.5 2.0 %shard_map.36.refs_0_ = f32[2,16,16,128]{3,2,1,0:T(8,128)S(1)} custom-call(f32[1,16,16,128]{3,2,1,0:T(8,128)S(1)} %get-tuple-element.34.t_in, f32[8,8,128]{2,1,0:T(8,128)S(1)} %fusion.3.e_in, f32[1,16,16,128]{3,2,1,0:T(8,128)S(1)} %get-tuple-element.37.f_in, f32[1,16,16,128]{3,2,1,0:T(8,128)S(1)} %get-tuple-element.38.w_in, ...), custom_call_target="tpu_custom_call" | custom-call | tf_op jit(solution)/shard_map/pallas_call | solution.py:235
  96.6 8.8 %shard_map.37.t_in = f32[2,24,24,128]{3,2,1,0:T(8,128)S(1)} custom-call(f32[2,16,16,128]{3,2,1,0:T(8,128)S(1)} %shard_map.36.refs_0_), custom_call_target="tpu_custom_call" | custom-call | tf_op jit(solution)/shard_map/pallas_call | solution.py:434
  105.4 5.5 %shard_map.38.t_in = f32[4,32,32,128]{3,2,1,0:T(8,128)S(1)} custom-call(f32[2,24,24,128]{3,2,1,0:T(8,128)S(1)} %shard_map.37.t_in, f32[2,24,24,128]{3,2,1,0:T(8,128)S(1)} %get-tuple-element.40.f_in, f32[2,24,24,128]{3,2,1,0:T(8,128)S(1)} %get-tuple-element.41.w_in, f32[4,32,32,128]{3,2,1,0:T(8,128)S(1)} %get-tuple-element.42.fine), custom_call_target="tpu_custom_call" | custom-call | tf_op jit(solution)/shard_map/pallas_call | solution.py:235
  110.9 28.6 %shard_map.39 = f32[4,32,32,128]{3,2,1,0:T(8,128)S(1)} custom-call(f32[4,32,32,128]{3,2,1,0:T(8,128)S(1)} %shard_map.38.t_in, f32[4,40,40,128]{3,2,1,0:T(8,128)} %get-tuple-element.43.f_in, f32[4,40,40,128]{3,2,1,0:T(8,128)} %get-tuple-element.44.w_in), custom_call_target="tpu_custom_call" | custom-call | tf_op jit(solution)/shard_map/pallas_call | solution.py:434
  139.5 1.3 copy.4
  (1 shorter events, 0.0 us)
Async XLA Ops:
  0.0 1.6 %copy-start = (f32[4,32,32,128]{3,2,1,0:T(8,128)S(1)}, f32[4,32,32,128]{3,2,1,0:T(8,128)}, u32[]{:S(2)}) copy-start(f32[4,32,32,128]{3,2,1,0:T(8,128)} %refs_1_.1) | copy-start | bytes 6291460
  1.6 1.6 %copy-start.1 = (f32[4,32,32,128]{3,2,1,0:T(8,128)S(1)}, f32[4,32,32,128]{3,2,1,0:T(8,128)}, u32[]{:S(2)}) copy-start(f32[4,32,32,128]{3,2,1,0:T(8,128)} %refs_0_.1) | copy-start | bytes 6291460
